TPU v7x, 32 devices: a whole 2x2x4 slice. The times are simulated.
32 devices in a mesh: ctx: 8 (over y, x, core), ch: 4 (over z).
Axes of the slice: x: 2, y: 2, z: 4, core: 2. Of those that a mesh axis runs over, the one named last changes fastest.
Arguments:
- projected: bfloat16 [1024, 3, 8192], P('ctx', None, 'ch'), may hold values from -6 to 6
- short_filter: float32 [3, 3, 8192], P(None, None, 'ch'), may hold values from -2.5 to 2.5
- decay_rate: float32 [16, 8192], P(None, 'ch'), as said below
- residue: float32 [16, 8192], P(None, 'ch'), as said below
- skip: float32 [8192], P('ch'), may hold values from -4 to 4
- state_in: float32 [16, 8192], P(None, 'ch'), as said below
- out_weight: bfloat16 [8192, 8192], P('ch'), may hold values from -0.09375 to 0.09375
- cotangent: bfloat16 [1024, 8192], P('ctx', 'ch'), may hold values from -6 to 6
Outputs:
- mixed_out: bfloat16 [1024, 8192], P('ctx', 'ch')
- grad_projected: bfloat16 [1024, 3, 8192], P('ctx', None, 'ch')
- grad_weight: bfloat16 [8192, 8192], P('ctx', 'ch')
- grad_filter: float32 [3, 3, 8192], P(None, None, 'ch')
- grad_residue: float32 [16, 8192], P(None, 'ch')
- grad_skip: float32 [8192], P('ch')
- grad_state: float32 [16, 8192], P(None, 'ch')
Inputs may be any that keep to these rules, and one draw needn't show every extreme that they name: `decay_rate`: every rate lies between 0.1 / 1024 and 0.05. `residue`: residues are real numbers of either sign. `state_in`: state entries are real numbers of either sign.
All inputs are finite; a program needn't handle non-finite values.
Results may differ from a plain program's by a relative error of at most 0.019.
Values may be sent and summed in bfloat16 or wider, within the bound.
A program may use at most 256 MiB of HBM per device.

v0:
```python
import jax
import jax.numpy as jnp
from jax import lax
from jax.sharding import PartitionSpec as P

HIGHEST = lax.Precision.HIGHEST


def shifted(block, axis, distance):
    devices = range(lax.axis_size(axis))
    route = [(i - distance, i) for i in devices if i - distance in devices]
    return lax.ppermute(block, axis, route)


def block_length(tok_rows):
    return min(64, tok_rows)


def state_before(dev_decay, local_total, state_in):
    leading = lax.axis_index("ctx") == 0

    def state_relay(counter, current):
        arrived = shifted(
            (dev_decay * current + local_total).astype(jnp.bfloat16), "ctx", 1
        ).astype(jnp.float32)
        return jnp.where(leading, state_in, arrived)

    opening = jnp.where(leading, state_in, jnp.zeros_like(state_in))
    return lax.fori_loop(0, lax.axis_size("ctx") - 1, state_relay, opening)


def adjoint_after(dev_decay, local_first):

    def adjoint_relay(counter, current):
        return shifted((dev_decay * current + local_first).astype(jnp.bfloat16), "ctx", -1).astype(
            jnp.float32
        )

    return lax.fori_loop(0, lax.axis_size("ctx") - 1, adjoint_relay, jnp.zeros_like(local_first))


def on_device(projected, short_filter, decay_rate, residue, skip, state_in, out_weight, cotangent):
    tok_rows = projected.shape[0]
    chan_count = projected.shape[2]
    mode_count = decay_rate.shape[0]
    taps = short_filter.shape[1]
    rim_rows = taps - 1
    block_rows = block_length(tok_rows)
    block_count = tok_rows // block_rows
    position = lax.axis_index("ctx").astype(jnp.float32)
    before = shifted(projected[tok_rows - rim_rows :], "ctx", 1)
    padded = jnp.concatenate([before, projected], 0).astype(jnp.float32)
    featurized = padded[rim_rows:] * short_filter[None, :, 0, :]
    for offset in range(1, taps):
        featurized = (
            featurized
            + padded[rim_rows - offset : rim_rows - offset + tok_rows]
            * short_filter[None, :, offset, :]
        )
    query = featurized[:, 0]
    keyed = featurized[:, 1]
    valued = featurized[:, 2]
    product = keyed * valued
    lag_ids = jnp.arange(block_rows)
    powers = jnp.exp(-decay_rate[None] * lag_ids.astype(jnp.float32)[:, None, None])
    pole = jnp.exp(-decay_rate)
    across = jnp.exp(-decay_rate * block_rows)
    kernel = jnp.einsum("lmc,mc->lc", powers, residue, precision=HIGHEST)
    difference = lag_ids[:, None] - lag_ids[None, :]
    causal = (difference >= 0)[:, :, None]
    toeplitz = jnp.where(causal, jnp.take(kernel, jnp.maximum(difference, 0), axis=0), 0.0)
    source_blocks = product.reshape(block_count, block_rows, chan_count)
    inner = jnp.einsum("ijc,kjc->kic", toeplitz, source_blocks, precision=HIGHEST)
    block_ends = jnp.einsum("jmc,kjc->kmc", powers[::-1], source_blocks, precision=HIGHEST)

    def run_forward(carry, item):
        return (across * carry + item, carry)

    local_total, local_starts = lax.scan(
        run_forward, jnp.zeros((mode_count, chan_count), jnp.float32), block_ends
    )
    dev_decay = jnp.exp(-decay_rate * tok_rows)
    incoming = state_before(dev_decay, local_total, state_in)
    block_decay = jnp.exp(
        -decay_rate[None] * (block_rows * jnp.arange(block_count, dtype=jnp.float32))[:, None, None]
    )
    starts = local_starts + block_decay * incoming[None]
    lifted = residue[None] * powers * pole[None]
    carried = jnp.einsum("imc,kmc->kic", lifted, starts, precision=HIGHEST)
    long_mix = (inner + carried).reshape(tok_rows, chan_count)
    combined = long_mix + skip[None] * product
    gated = (query * combined).astype(jnp.bfloat16)
    partial_out = jnp.dot(gated, out_weight, preferred_element_type=jnp.float32)
    mixed_out = lax.psum_scatter(
        partial_out.astype(jnp.bfloat16), "ch", scatter_dimension=1, tiled=True
    )
    gathered = lax.all_gather(cotangent, "ch", axis=1, tiled=True)
    grad_gated = lax.dot_general(
        gathered, out_weight, (((1,), (1,)), ((), ())), preferred_element_type=jnp.float32
    )
    columns = lax.all_to_all(gathered, "ctx", split_axis=1, concat_axis=0, tiled=True)
    piece = lax.all_gather(gated, "ctx", axis=0, tiled=True)
    shard_count = piece.shape[0] // tok_rows
    terms = jnp.einsum(
        "nte,ntc->nec",
        columns.reshape(shard_count, tok_rows, columns.shape[1]),
        piece.reshape(shard_count, tok_rows, chan_count),
        preferred_element_type=jnp.float32,
    )
    rounded = lax.optimization_barrier(terms.astype(jnp.bfloat16)).astype(jnp.float32)
    weight_sum = jnp.sum(rounded, 0)
    grad_weight = weight_sum.astype(jnp.bfloat16)
    grad_query = grad_gated * combined
    grad_combined = grad_gated * query
    skip_part = jnp.sum(grad_combined * product, 0)
    grad_blocks = grad_combined.reshape(block_count, block_rows, chan_count)
    inner_back = jnp.einsum("ijc,kic->kjc", toeplitz, grad_blocks, precision=HIGHEST)
    block_firsts = jnp.einsum("imc,kic->kmc", powers, grad_blocks, precision=HIGHEST)

    def run_backward(carry, item):
        return (across * carry + item, carry)

    local_first, local_next = lax.scan(
        run_backward, jnp.zeros((mode_count, chan_count), jnp.float32), block_firsts, reverse=True
    )
    beyond = adjoint_after(dev_decay, local_first)
    tail_decay = jnp.exp(
        -decay_rate[None]
        * (block_rows * (block_count - 1 - jnp.arange(block_count, dtype=jnp.float32)))[
            :, None, None
        ]
    )
    next_firsts = local_next + tail_decay * beyond[None]
    back_lift = residue[None] * powers[::-1] * pole[None]
    carried_back = jnp.einsum("jmc,kmc->kjc", back_lift, next_firsts, precision=HIGHEST)
    grad_product = (inner_back + carried_back).reshape(tok_rows, chan_count) + skip[
        None
    ] * grad_combined
    head_terms = jnp.einsum("imc,kic->kmc", lifted / residue[None], grad_blocks, precision=HIGHEST)
    residue_part = jnp.sum(head_terms * starts, 0)
    crossed = jnp.einsum("kic,kjc->ijc", grad_blocks, source_blocks, precision=HIGHEST)
    lag_values = jnp.maximum(difference, 0).astype(jnp.float32)

    def per_mode(rates):
        decays = jnp.where(causal, jnp.exp(-rates[None, None] * lag_values[:, :, None]), 0.0)
        return jnp.sum(decays * crossed, (0, 1))

    residue_part = residue_part + lax.map(per_mode, decay_rate)
    leading_part = jnp.exp(-decay_rate * (tok_rows * position)) * local_first
    grad_featurized = jnp.stack([grad_query, grad_product * valued, grad_product * keyed], 1)
    after = shifted(grad_featurized[:rim_rows], "ctx", -1)
    extended = jnp.concatenate([grad_featurized, after], 0)
    grad_streams = extended[:tok_rows] * short_filter[None, :, 0, :]
    for offset in range(1, taps):
        grad_streams = (
            grad_streams + extended[offset : offset + tok_rows] * short_filter[None, :, offset, :]
        )
    grad_projected = grad_streams.astype(jnp.bfloat16)
    filter_part = jnp.stack(
        [
            jnp.sum(grad_featurized * padded[rim_rows - offset : rim_rows - offset + tok_rows], 0)
            for offset in range(taps)
        ],
        1,
    )
    grad_filter, grad_residue, grad_skip, first_adjoint = (
        lax.psum(filter_part.astype(jnp.bfloat16), "ctx").astype(jnp.float32),
        lax.psum(residue_part.astype(jnp.bfloat16), "ctx").astype(jnp.float32),
        lax.psum(skip_part.astype(jnp.bfloat16), "ctx").astype(jnp.float32),
        lax.psum(leading_part.astype(jnp.bfloat16), "ctx").astype(jnp.float32),
    )
    grad_state = residue * pole * first_adjoint
    return (
        mixed_out,
        grad_projected,
        grad_weight,
        grad_filter,
        grad_residue,
        grad_skip,
        grad_state,
    )


def solution(mesh):
    in_specs = (
        P("ctx", None, "ch"),
        P(None, None, "ch"),
        P(None, "ch"),
        P(None, "ch"),
        P("ch"),
        P(None, "ch"),
        P("ch", None),
        P("ctx", "ch"),
    )
    out_specs = (
        P("ctx", "ch"),
        P("ctx", None, "ch"),
        P("ctx", "ch"),
        P(None, None, "ch"),
        P(None, "ch"),
        P("ch"),
        P(None, "ch"),
    )
    return jax.shard_map(
        on_device, mesh=mesh, in_specs=in_specs, out_specs=out_specs, check_vma=False
    )
```

profile of v0, /device:TPU:0, one launch (start us, length us, event | category | flops | bytes accessed | tf_op | source)
XLA Modules:
  0.0 1197.8 jit_solution(16417387735599015198)
XLA Ops:
  46.0 23.8 %gather_fusion = f32[4096,2048]{1,0:T(8,128)} fusion(f32[64,2048]{1,0:T(8,128)S(1)} %bitcast.146, s32[4096]{0:T(1024)S(1)} %broadcast_clamp_fusion), kind=kCustom, calls=%fused_computation | custom fusion | bytes 67125248 | tf_op jit(solution)/shard_map/jit(_take)/gather | solution.py:71
  69.8 58.9 %copy.106 = f32[64,64,2048]{1,0,2:T(8,128)} copy(f32[64,64,2048]{2,1,0:T(8,128)} %bitcast.147) | data formatting | bytes 67108864 | tf_op jit(solution)/shard_map/jit(_take)/gather | solution.py:71
  128.7 25.0 %rev.4 = f32[64,16,2048]{0,1,2:T(8,128)} reverse(f32[64,16,2048]{0,1,2:T(8,128)} %multiply_exponential_fusion), dimensions={0} | reverse | bytes 16777216 | tf_op jit(solution)/shard_map/rev | solution.py:74
  159.4 29.7 %convolution_bitcast_fusion.1 = f32[2,16,2048]{1,0,2:T(2,128)} fusion(f32[2,64,2048]{1,0,2:T(2,128)S(1)} %copy.107, f32[64,16,2048]{0,1,2:T(8,128)} %rev.4), kind=kOutput, calls=%fused_computation.69 | convolution fusion | flops 50331648 | bytes 9699328 | tf_op jit(solution)/shard_map/jmc,kjc->kmc/dot_general | solution.py:74
  192.2 109.8 %fusion.8 = f32[2048,2,64]{2,1,0:T(2,128)} fusion(f32[2,64,2048]{1,0,2:T(2,128)S(1)} %copy.107, f32[64,64,2048]{1,0,2:T(8,128)} %copy.106, pred[64,64]{1,0:T(8,128)(4,1)S(1)} %get-tuple-element.449, pred[64,64]{1,0:T(8,128)(4,1)S(1)} %get-tuple-element.450), kind=kOutput, calls=%fused_computation.19 | convolution fusion | flops 218103808 | bytes 35659776 | tf_op jit(solution)/shard_map/ijc,kjc->kic/dot_general | solution.py:73
  302.0 19.2 %multiply_reduce_fusion.5 = (bf16[2048]{0:T(1024)(128)(2,1)}, f32[128,2048]{1,0:T(8,128)S(1)}, f32[128,2048]{1,0:T(8,128)}) fusion(f32[128,3,2048]{2,0,1:T(8,128)} %copy-done.3, bf16[128,8192]{0,1:T(8,128)(2,1)} %all-gather.3.cloned.1.call-done, bf16[2048,8192]{1,0:T(8,128)(2,1)} %param.24), kind=kOutput, calls=%fused_computation.78 | convolution fusion | flops 4296013824 | bytes 40898560 | tf_op jit(solution)/shard_map/dot_general | solution.py:98
  323.8 30.1 %fusion.41 = f32[2,16,2048]{1,0,2:T(2,128)} fusion(f32[2,64,2048]{1,0,2:T(2,128)} %copy.115, f32[64]{0:T(128)S(1)} %copy-done.38, f32[16,2048]{0,1:T(8,128)} %copy-done.15), kind=kOutput, calls=%fused_computation.68 | convolution fusion | flops 52428800 | bytes 1442048 | tf_op jit(solution)/shard_map/imc,kic->kmc/dot_general | solution.py:118
  353.9 60.8 %fusion.7 = f32[2048,2,64]{2,1,0:T(2,128)} fusion(f32[2,64,2048]{1,0,2:T(2,128)S(1)} %copy-done.5, f32[64,64,2048]{1,0,2:T(8,128)} %copy.106, pred[64,64]{1,0:T(8,128)(4,1)S(1)} %get-tuple-element.449, pred[64,64]{1,0:T(8,128)(4,1)S(1)} %get-tuple-element.450), kind=kOutput, calls=%fused_computation.18 | convolution fusion | flops 218103808 | bytes 35659776 | tf_op jit(solution)/shard_map/ijc,kic->kjc/dot_general | solution.py:117
  414.7 109.7 %convolution_bitcast_fusion = f32[64,64,2048]{0,1,2:T(8,128)} fusion(f32[2,64,2048]{1,0,2:T(2,128)S(1)} %copy.107, f32[2,64,2048]{1,0,2:T(2,128)S(1)} %copy-done.5), kind=kOutput, calls=%fused_computation.29 | convolution fusion | flops 201326592 | bytes 35651584 | tf_op jit(solution)/shard_map/kic,kjc->ijc/dot_general | solution.py:141
  529.4 43.3 %fusion.23 = f32[2048,2,16]{2,1,0:T(2,128)} fusion(f32[2,64,2048]{1,0,2:T(2,128)S(1)} %copy-done.6, f32[16,2048]{0,1:T(8,128)} %copy.111, f32[16,2048]{0,1:T(8,128)} %copy.110, f32[64]{0:T(128)S(1)} %copy-done.39, f32[16,2048]{0,1:T(8,128)} %copy-done.15), kind=kOutput, calls=%fused_computation.39 | convolution fusion | flops 58720256 | bytes 1704192 | tf_op jit(solution)/shard_map/imc,kic->kmc/dot_general | solution.py:139
  575.4 36.5 %while.67 = (s32[]{:T(128)}, f32[16,2048]{1,0:T(8,128)S(1)}, pred[]{:T(512)}, f32[16,2048]{1,0:T(8,128)S(1)}, f32[16,2048]{1,0:T(8,128)S(1)}, /*index=5*/f32[16,2048]{1,0:T(8,128)S(1)}) while((s32[]{:T(128)}, f32[16,2048]{1,0:T(8,128)S(1)}, pred[]{:T(512)}, f32[16,2048]{1,0:T(8,128)S(1)}, f32[16,2048]{1,0:T(8,128)S(1)}, ...), condition=%wide.region_3.4_spmd.clone, body=%wide.region_2.3_spmd.sunk.clone | while | flops 163842 | bytes 1048686 | solution.py:29
  612.0 46.4 %while.71 = (s32[]{:T(128)}, f32[16,2048]{1,0:T(8,128)S(1)}, f32[16,2048]{1,0:T(8,128)S(1)}, f32[16,2048]{1,0:T(8,128)S(1)}) while((s32[]{:T(128)}, f32[16,2048]{1,0:T(8,128)S(1)}, f32[16,2048]{1,0:T(8,128)S(1)}, f32[16,2048]{1,0:T(8,128)S(1)}) %tuple.183), condition=%wide.region_8.9_spmd.clone.clone, body=%wide.region_7.8_spmd.clone.sunk.clone | while | flops 163843 | bytes 917607 | solution.py:39
  661.8 33.1 %add_bitcast_fusion.1 = f32[2,64,2048]{1,0,2:T(2,128)} fusion(f32[2048,2,64]{2,1,0:T(2,128)} %fusion.8, f32[2,16,2048]{1,0,2:T(2,128)S(1)} %copy.112, f32[16,2048]{0,1:T(8,128)} %copy.111, f32[16,2048]{0,1:T(8,128)} %copy.110, f32[64]{0:T(128)S(1)} %copy-done.39, f32[16,2048]{0,1:T(8,128)S(1)} %copy-done.16), kind=kOutput, calls=%fused_computation.66 | convolution fusion | flops 56885248 | bytes 2752768 | tf_op jit(solution)/shard_map/imc,kmc->kic/dot_general | solution.py:89
  702.8 23.7 %add_bitcast_fusion = f32[2,64,2048]{1,0,2:T(2,128)} fusion(f32[2048,2,64]{2,1,0:T(2,128)S(1)} %copy-done.17, f32[2,16,2048]{1,0,2:T(2,128)} %copy.118, f32[64,16,2048]{0,1,2:T(8,128)} %rev.4, f32[16,2048]{0,1:T(8,128)} %copy.111, f32[16,2048]{0,1:T(8,128)S(1)} %copy-done.28), kind=kOutput, calls=%fused_computation.65 | convolution fusion | flops 54788096 | bytes 11010048 | tf_op jit(solution)/shard_map/jmc,kmc->kjc/dot_general | solution.py:135
  730.4 50.9 %copy.127 = f32[64,64,2048]{2,1,0:T(8,128)} copy(f32[64,64,2048]{0,1,2:T(8,128)} %convolution_bitcast_fusion) | data formatting | bytes 67108864
  781.3 257.9 %while.68 = (s32[]{:T(128)}, f32[16,2048]{1,0:T(8,128)}, f32[16,2048]{1,0:T(8,128)S(1)}, f32[64,64,2048]{2,1,0:T(8,128)}) while((s32[]{:T(128)}, f32[16,2048]{1,0:T(8,128)}, f32[16,2048]{1,0:T(8,128)S(1)}, f32[64,64,2048]{2,1,0:T(8,128)}) %tuple.184), condition=%wide.region_17.18_spmd.clone.clone, body=%wide.region_15.17_spmd.clone.sunk.clone | while | flops 33574912 | bytes 33644612 | solution.py:148
  781.4 14.7 %multiply_reduce_fusion.8 = f32[2048]{0:T(1024)S(1)} fusion(f32[64,64,2048]{2,1,0:T(8,128)} %get-tuple-element.735, f32[64,64]{1,0:T(8,128)S(1)} %maximum_convert_fusion.4, f32[2048]{0:T(1024)S(1)} %bitcast.154, pred[64,64]{1,0:T(8,128)(4,1)S(1)} %fusion.80), kind=kLoop, calls=%fused_computation.5.clone.1.clone | loop fusion | flops 33552384 | bytes 33591296 | tf_op jit(solution)/shard_map/while/body/eval_jaxpr/reduce_sum | solution.py:146
  797.6 14.6 %multiply_reduce_fusion.8 = f32[2048]{0:T(1024)S(1)} fusion(f32[64,64,2048]{2,1,0:T(8,128)} %get-tuple-element.735, f32[64,64]{1,0:T(8,128)S(1)} %maximum_convert_fusion.4, f32[2048]{0:T(1024)S(1)} %bitcast.154, pred[64,64]{1,0:T(8,128)(4,1)S(1)} %fusion.80), kind=kLoop, calls=%fused_computation.5.clone.1.clone | loop fusion | flops 33552384 | bytes 33591296 | tf_op jit(solution)/shard_map/while/body/eval_jaxpr/reduce_sum | solution.py:146
  813.7 14.6 %multiply_reduce_fusion.8 = f32[2048]{0:T(1024)S(1)} fusion(f32[64,64,2048]{2,1,0:T(8,128)} %get-tuple-element.735, f32[64,64]{1,0:T(8,128)S(1)} %maximum_convert_fusion.4, f32[2048]{0:T(1024)S(1)} %bitcast.154, pred[64,64]{1,0:T(8,128)(4,1)S(1)} %fusion.80), kind=kLoop, calls=%fused_computation.5.clone.1.clone | loop fusion | flops 33552384 | bytes 33591296 | tf_op jit(solution)/shard_map/while/body/eval_jaxpr/reduce_sum | solution.py:146
  829.9 14.6 %multiply_reduce_fusion.8 = f32[2048]{0:T(1024)S(1)} fusion(f32[64,64,2048]{2,1,0:T(8,128)} %get-tuple-element.735, f32[64,64]{1,0:T(8,128)S(1)} %maximum_convert_fusion.4, f32[2048]{0:T(1024)S(1)} %bitcast.154, pred[64,64]{1,0:T(8,128)(4,1)S(1)} %fusion.80), kind=kLoop, calls=%fused_computation.5.clone.1.clone | loop fusion | flops 33552384 | bytes 33591296 | tf_op jit(solution)/shard_map/while/body/eval_jaxpr/reduce_sum | solution.py:146
  846.0 14.6 %multiply_reduce_fusion.8 = f32[2048]{0:T(1024)S(1)} fusion(f32[64,64,2048]{2,1,0:T(8,128)} %get-tuple-element.735, f32[64,64]{1,0:T(8,128)S(1)} %maximum_convert_fusion.4, f32[2048]{0:T(1024)S(1)} %bitcast.154, pred[64,64]{1,0:T(8,128)(4,1)S(1)} %fusion.80), kind=kLoop, calls=%fused_computation.5.clone.1.clone | loop fusion | flops 33552384 | bytes 33591296 | tf_op jit(solution)/shard_map/while/body/eval_jaxpr/reduce_sum | solution.py:146
  1045.9 16.7 %convolution_convert_fusion = bf16[128,8192]{1,0:T(8,128)(2,1)} fusion(bf16[128,2048]{1,0:T(8,128)(2,1)} %get-tuple-element.433, bf16[2048,8192]{1,0:T(8,128)(2,1)} %param.24), kind=kOutput, calls=%fused_computation.40 | convolution fusion | flops 4296015872 | bytes 36175872 | tf_op jit(solution)/shard_map/dot_general | solution.py:93
  1086.4 39.8 %all-reduce = (bf16[3,3,2048]{2,0,1:T(4,128)(2,1)S(1)}, bf16[2048]{0:T(1024)(128)(2,1)S(1)}) all-reduce(bf16[3,3,2048]{2,0,1:T(4,128)(2,1)S(1)} %pad_maximum_fusion.2, bf16[2048]{0:T(1024)(128)(2,1)S(1)} %copy-done.35), channel_id=1, replica_groups=mesh['ctx'=8,'ch'=4] {'ctx'}, use_global_device_ids=true, to_apply=%region_13.14 | all-reduce | flops 20480 | bytes 81920 | tf_op jit(solution)/shard_map/psum | solution.py:167
  1144.4 16.2 %convert_bitcast_fusion = bf16[8,1024,2048]{1,2,0:T(8,128)(2,1)} fusion(bf16[8,128,2048]{2,1,0:T(8,128)(2,1)} %bitcast.150, bf16[128,8,1024]{2,0,1:T(8,128)(2,1)} %all-to-all-done), kind=kOutput, calls=%fused_computation.20 | convolution fusion | flops 4311744512 | bytes 39845888 | tf_op jit(solution)/shard_map/nte,ntc->nec/dot_general | solution.py:104
  (297 shorter events, 419.1 us)
Async XLA Ops:
  7.2 294.8 %all-gather.3.cloned.1.call-start = ((), (), s32[]{:S(2)}) async-start(), calls=%async_computation.3 | async-start | bytes 2621440 | tf_op jit(solution)/shard_map/all_gather | solution.py:97
  8.7 145.0 %collective-permute-start.2 = (bf16[2,3,2048]{2,0,1:T(2,128)(2,1)}, bf16[2,3,2048]{2,0,1:T(2,128)(2,1)}, u32[]{:S(2)}, u32[]{:S(2)}) collective-permute-start(bf16[2,3,2048]{2,0,1:T(2,128)(2,1)} %slice.45), channel_id=1, source_target_pairs={{0,4},{4,8},{8,12},{12,16},{16,20},{20,24},{24,28},{1,5},{5,9},{9,... | collective-permute-start | bytes 73736 | tf_op jit(solution)/shard_map/ppermute | solution.py:12
  13.8 1113.7 %all-reduce.4.cloned.1.call-start = ((), (), s32[]{:S(2)}) async-start(), calls=%async_computation.5 | async-start | bytes 262144 | tf_op jit(solution)/shard_map/psum | solution.py:168
  42.3 112.7 %copy-start.29 = (f32[3,2048]{1,0:T(4,128)}, f32[3,2048]{1,0:T(4,128)S(1)}, u32[]{:S(2)}) copy-start(f32[3,2048]{1,0:T(4,128)S(1)} %get-tuple-element.447) | copy-start | bytes 73732
  575.5 4.9 collective-permute-start
  580.5 3.2 collective-permute-start
  583.8 5.6 collective-permute-start
  589.4 5.6 collective-permute-start
  595.1 5.6 collective-permute-start
  600.7 5.6 collective-permute-start
  606.4 5.6 collective-permute-start
  612.0 5.6 collective-permute-start.1
  617.7 7.3 collective-permute-start.1
  625.1 6.3 collective-permute-start.1
  631.5 7.2 collective-permute-start.1
  638.8 6.5 collective-permute-start.1
  645.3 6.5 collective-permute-start.1
  651.9 6.5 collective-permute-start.1
  781.3 259.5 %copy-start.4 = (f32[128,3,2048]{2,0,1:T(8,128)S(1)}, f32[128,3,2048]{2,0,1:T(8,128)}, u32[]{:S(2)}) copy-start(f32[128,3,2048]{2,0,1:T(8,128)} %copy-done.3) | copy-start | bytes 9437188
  781.3 259.5 %copy-start.36 = (f32[2048]{0:T(1024)S(1)}, f32[2048]{0:T(1024)}, u32[]{:S(2)}) copy-start(f32[2048]{0:T(1024)} %param.22) | copy-start | bytes 24580
  1040.8 103.6 %all-gather.5.cloned.1.call-start = ((), (), s32[]{:S(2)}) async-start(), calls=%async_computation.4 | async-start | bytes 4718592 | tf_op jit(solution)/shard_map/all_gather | solution.py:102
  1045.7 145.4 %reduce-scatter.2.cloned.1.call-start = ((), (), s32[]{:S(2)}) async-start(), calls=%async_computation.2 | async-start | bytes 2621440 | tf_op jit(solution)/shard_map/reduce_scatter | solution.py:94
  1062.9 18.5 %collective-permute-start.3 = (f32[2,3,2048]{2,0,1:T(2,128)S(1)}, f32[2,3,2048]{2,0,1:T(2,128)S(1)}, u32[]{:S(2)}, u32[]{:S(2)}) collective-permute-start(f32[2,3,2048]{2,0,1:T(2,128)S(1)} %slice.66), channel_id=1, source_target_pairs={{4,0},{8,4},{12,8},{16,12},{20,16},{24,20},{28,24},{5,1},{9,5},{13... | collective-permute-start | bytes 147464 | tf_op jit(solution)/shard_map/ppermute | solution.py:12
  1068.2 62.4 %all-to-all-start = ((bf16[128,8,1024]{2,0,1:T(8,128)(2,1)}), bf16[128,8,1024]{2,0,1:T(8,128)(2,1)}, u32[]{:S(2)}, u32[]{:S(2)}) async-start(bf16[128,8,1024]{2,0,1:T(8,128)(2,1)} %copy.120), calls=%async_computation.1 | async-start | bytes 4194304 | tf_op jit(solution)/shard_map/all_to_all | solution.py:101
  (39 other events, 1330.4 us)
Sparse Core Ops, SparseCore 0:
  13.9 47.9 all-gather.2
  1040.9 65.3 all-reduce.3
  1108.4 35.9 all-gather.4
  1147.2 43.8 reduce-scatter.1
where the time goes:
time: 1220 us; the launch traced here: 1200 us
  matrix products  492 us (40%)
  other arithmetic  291 us (24%)
  local copies, waits for them, and re-layouts  236 us (19%)
  waiting for transfers between devices  66.5 us (5%)
  starting transfers between devices  56.8 us (5%)
  blocking collectives  39.8 us (3%)
  between operations  14.6 us (1%)
    reduce_sum x16, other arithmetic, per_mode(): return jnp.sum(decays * crossed, (0, 1))  233 us
    dot_general x1, matrix products, on_device(): jnp.einsum('ijc,kjc->kic', toeplitz, source_blocks, precision=HIGHEST)  110 us
    dot_general x1, matrix products, on_device(): jnp.einsum('kic,kjc->ijc', grad_blocks, source_blocks, precision=HIGHEST)  110 us
    gather x2, local copies, waits for them, and re-layouts, on_device(): jnp.take(kernel, jnp.maximum(difference, 0), axis=0)  82.7 us
    unnamed x94, local copies, waits for them, and re-layouts  73.9 us
    dot_general x1, matrix products, on_device(): jnp.einsum('ijc,kic->kjc', toeplitz, grad_blocks, precision=HIGHEST)  60.8 us
    ppermute x16, starting transfers between devices, shifted(): return lax.ppermute(block, axis, route)  43.3 us
    dot_general x1, matrix products, on_device(): jnp.einsum('imc,kic->kmc', lifted / residue[None], grad_blocks, precision...  43.3 us
  transfers between devices with their start and end apart: 21, of which 16 were waited for; matrix products, arithmetic and copies ran while one was open for 30% of the time, Pallas kernels for 0%

commit v1 on v0

v1 whole, which is shorter than its diff:
```python
import functools

import jax
import jax.numpy as jnp
from jax import lax
from jax.experimental import pallas as pl
from jax.experimental.pallas import tpu as pltpu
from jax.sharding import PartitionSpec as P

LANES = 128
SUB = 8
UNROLL = 4
VMEM_BYTES = 40 * 1024 * 1024
F32 = jnp.float32
BF16 = jnp.bfloat16


def shifted(block, axis, distance):
    devices = range(lax.axis_size(axis))
    route = [(i - distance, i) for i in devices if i - distance in devices]
    return lax.ppermute(block, axis, route)


def tile(token, rows, half):
    return pl.ds(pl.multiple_of(token * rows + half * SUB, SUB), SUB)


def part(half):
    return slice(half * SUB, (half + 1) * SUB)


def to_tiles(source, store, tokens, rows):
    def chunk(index, carry):
        first = pl.multiple_of(index * SUB, SUB)
        for group in range(rows):
            store(pl.ds(first * rows + group, SUB, stride=rows), source(first, group))
        return carry

    lax.fori_loop(0, tokens // SUB, chunk, 0)


def from_tiles(load, store, tokens, rows):
    step = 2 * SUB

    def chunk(index, carry):
        first = pl.multiple_of(index * step, step)
        for group in range(rows):
            store(first, group, load(pl.ds(first * rows + group, step, stride=rows)))
        return carry

    lax.fori_loop(0, tokens // step, chunk, 0)


def lanes(group):
    return slice(group * LANES, (group + 1) * LANES)


class Params:
    def __init__(self, ref, streams, taps, modes):
        self.ref, self.streams, self.taps, self.modes = ref, streams, taps, modes
        self.first = streams * taps

    def filters(self, stream, half):
        return [self.ref[stream * self.taps + s, part(half), :] for s in range(self.taps)]

    def decay(self, m, half):
        return self.ref[self.first + m, part(half), :]

    def residue(self, m, half):
        return self.ref[self.first + self.modes + m, part(half), :]

    def state_in(self, m, half):
        return self.ref[self.first + 2 * self.modes + m, part(half), :]

    def skip(self, half):
        return self.ref[self.first + 3 * self.modes, part(half), :]


def featurize(tiles_ref, filters, stream, token, rows, half, taps):
    total = None
    for s in range(taps):
        term = filters[s] * tiles_ref[stream, tile(token + taps - 1 - s, rows, half), :]
        total = term if total is None else total + term
    return total


def tree_sum(terms):
    while len(terms) > 1:
        terms = [sum(terms[i : i + 2][1:], terms[i]) for i in range(0, len(terms), 2)]
    return terms[0]


def total_kernel(dims, ext_ref, params_ref, tiles_ref, total_ref, keep):
    tokens, rows, modes, streams, taps = dims
    params = Params(params_ref, streams, taps, modes)
    for j in range(streams):

        def store(where, value, j=j):
            tiles_ref[j, where, :] = value

        to_tiles(
            lambda first, group, j=j: ext_ref[j, pl.ds(first, SUB), lanes(group)],
            store,
            ext_ref.shape[1],
            rows,
        )
    for half in range(rows // SUB):
        filters = [params.filters(j, half) for j in range(streams)]
        poles = [jnp.exp(-params.decay(m, half)) for m in range(modes)]

        def steps(index, states):
            for u in range(UNROLL):
                t = index * UNROLL + u
                product = featurize(
                    tiles_ref, filters[1], 1, t, rows, half, taps
                ) * featurize(tiles_ref, filters[2], 2, t, rows, half, taps)
                states = [p * s + product for p, s in zip(poles, states)]
            return states

        states = lax.fori_loop(
            0, tokens // UNROLL, steps, [jnp.zeros((SUB, LANES), F32)] * modes
        )
        for m in range(modes):
            keep[m, part(half), :] = states[m]
    total_ref[...] = keep[...].astype(BF16)


def forward_kernel(
    dims, count, pos_ref, tiles_ref, params_ref, totals_ref, gated_ref, combined_ref, gated_keep
):
    tokens, rows, modes, streams, taps = dims
    params = Params(params_ref, streams, taps, modes)
    position = pos_ref[0]
    for half in range(rows // SUB):
        filters = [params.filters(j, half) for j in range(streams)]
        poles = [jnp.exp(-params.decay(m, half)) for m in range(modes)]
        skip = params.skip(half)
        states = []
        for m in range(modes):
            across = jnp.exp(-params.decay(m, half) * tokens)
            state = params.state_in(m, half)
            for j in range(count - 1):
                arrived = totals_ref[j, m].astype(F32)[part(half)]
                state = jnp.where(j < position, across * state + arrived, state)
            states.append(state)

        def advance(t, states, gate):
            keyed = featurize(tiles_ref, filters[1], 1, t, rows, half, taps)
            valued = featurize(tiles_ref, filters[2], 2, t, rows, half, taps)
            product = keyed * valued
            states = [p * s + product for p, s in zip(poles, states)]
            mix = tree_sum([params.residue(m, half) * states[m] for m in range(modes)])
            combined = mix + skip * product
            combined_ref[tile(t, rows, half), :] = combined
            if gate:
                query = featurize(tiles_ref, filters[0], 0, t, rows, half, taps)
                gated_keep[tile(t, rows, half), :] = query * combined
            return states

        def steps(index, states):
            for u in range(UNROLL):
                states = advance(index * UNROLL + u, states, True)
            return states

        states = lax.fori_loop(0, tokens // UNROLL, steps, states)
        for extra in range(taps - 1):
            states = advance(tokens + extra, states, False)

    def store(first, group, value):
        gated_ref[pl.ds(first, 2 * SUB), lanes(group)] = value.astype(BF16)

    from_tiles(lambda where: gated_keep[where, :], store, tokens, rows)


def first_kernel(dims, grad_ref, tiles_ref, params_ref, grad_tiles_ref, first_ref, keep):
    tokens, rows, modes, streams, taps = dims
    params = Params(params_ref, streams, taps, modes)

    def store(where, value):
        grad_tiles_ref[where, :] = value

    to_tiles(
        lambda first, group: grad_ref[pl.ds(first, SUB), lanes(group)], store, tokens, rows
    )
    for half in range(rows // SUB):
        filters = params.filters(0, half)
        poles = [jnp.exp(-params.decay(m, half)) for m in range(modes)]

        def steps(index, states):
            for u in range(UNROLL):
                t = tokens - 1 - (index * UNROLL + u)
                query = featurize(tiles_ref, filters, 0, t, rows, half, taps)
                item = grad_tiles_ref[tile(t, rows, half), :] * query
                states = [p * s + item for p, s in zip(poles, states)]
            return states

        states = lax.fori_loop(
            0, tokens // UNROLL, steps, [jnp.zeros((SUB, LANES), F32)] * modes
        )
        for m in range(modes):
            keep[m, part(half), :] = states[m]
        for extra in range(taps - 1):
            keep[modes + extra, part(half), :] = grad_tiles_ref[tile(extra, rows, half), :]
    first_ref[...] = keep[...].astype(BF16)


def backward_kernel(
    dims,
    count,
    pos_ref,
    tiles_ref,
    params_ref,
    combined_ref,
    grad_ref,
    firsts_ref,
    stream_grad_ref,
    sums_ref,
    state_ref,
    feat_grad,
    sums,
):
    tokens, rows, modes, streams, taps = dims
    params = Params(params_ref, streams, taps, modes)
    position = pos_ref[0]
    follower = jnp.minimum(position + 1, count - 1)
    inside = position < count - 1
    for half in range(rows // SUB):
        filters = [params.filters(j, half) for j in range(streams)]
        poles = [jnp.exp(-params.decay(m, half)) for m in range(modes)]
        skip = params.skip(half)
        beyond = []
        for m in range(modes):
            across = jnp.exp(-params.decay(m, half) * tokens)
            adjoint = jnp.zeros((SUB, LANES), F32)
            mine = adjoint
            for j in reversed(range(count)):
                mine = jnp.where(position == j, adjoint, mine)
                adjoint = across * adjoint + firsts_ref[j, m].astype(F32)[part(half)]
            beyond.append(mine)
            lowered = poles[m] * adjoint
            state_ref[m, part(half), :] = params.residue(m, half) * lowered
            state_ref[modes + m, part(half), :] = params.state_in(m, half) * lowered

        def finish(t, adjoints, grad, grad_combined, keyed, valued):
            mix = tree_sum([params.residue(m, half) * adjoints[m] for m in range(modes)])
            grad_product = mix + skip * grad_combined
            where = tile(t, rows, half)
            feat_grad[0, where, :] = grad * combined_ref[where, :]
            feat_grad[1, where, :] = grad_product * valued
            feat_grad[2, where, :] = grad_product * keyed

        adjoints = beyond
        for extra in range(taps - 1):
            t = tokens + extra
            query, keyed, valued = [
                featurize(tiles_ref, filters[j], j, t, rows, half, taps) for j in range(streams)
            ]
            grad = firsts_ref[follower, modes + extra].astype(F32)[part(half)]
            grad = jnp.where(inside, grad, 0.0)
            grad_combined = grad * query
            finish(t, adjoints, grad, grad_combined, keyed, valued)
            if extra < taps - 2:
                adjoints = [
                    (a - grad_combined) * jnp.exp(params.decay(m, half))
                    for m, a in enumerate(adjoints)
                ]

        for m in range(modes):
            sums[m, part(half), :] = jnp.zeros((SUB, LANES), F32)

        def steps(index, adjoints):
            gathered = None
            for u in range(UNROLL):
                t = tokens - 1 - (index * UNROLL + u)
                query, keyed, valued = [
                    featurize(tiles_ref, filters[j], j, t, rows, half, taps)
                    for j in range(streams)
                ]
                grad = grad_ref[tile(t, rows, half), :]
                grad_combined = grad * query
                adjoints = [p * a + grad_combined for p, a in zip(poles, adjoints)]
                finish(t, adjoints, grad, grad_combined, keyed, valued)
                product = keyed * valued
                terms = [a * product for a in adjoints]
                gathered = terms if gathered is None else [g + x for g, x in zip(gathered, terms)]
            for m in range(modes):
                sums[m, part(half), :] += gathered[m]
            return adjoints

        lax.fori_loop(0, tokens // UNROLL, steps, beyond)

        def spread(index, totals):
            totals = list(totals)
            for u in range(UNROLL):
                t = index * UNROLL + u
                features = []
                for j in range(streams):
                    slices = [
                        tiles_ref[j, tile(t + taps - 1 - s, rows, half), :] for s in range(taps)
                    ]
                    grads = [feat_grad[j, tile(t + s, rows, half), :] for s in range(taps)]
                    features.append(sum(filters[j][s] * slices[s] for s in range(taps)))
                    for s in range(taps):
                        totals[j * taps + s] = totals[j * taps + s] + grads[0] * slices[s]
                    feat_grad[j, tile(t, rows, half), :] = sum(
                        filters[j][s] * grads[s] for s in range(taps)
                    )
                grad_combined = grad_ref[tile(t, rows, half), :] * features[0]
                totals[-1] = totals[-1] + grad_combined * (features[1] * features[2])
            return totals

        totals = lax.fori_loop(
            0,
            tokens // UNROLL,
            spread,
            [jnp.zeros((SUB, LANES), F32)] * (streams * taps + 1),
        )
        for index, value in enumerate(totals):
            sums[modes + index, part(half), :] = value

    for j in range(streams):

        def store(first, group, value, j=j):
            stream_grad_ref[j, pl.ds(first, 2 * SUB), lanes(group)] = value.astype(BF16)

        from_tiles(lambda where, j=j: feat_grad[j, where, :], store, tokens, rows)
    sums_ref[...] = sums[...].astype(BF16)


def call(kernel, outs, scratch, name, operands, scalar=False, flops=0):
    whole = pl.BlockSpec(memory_space=pltpu.VMEM)
    specs = [whole] * len(operands)
    if scalar:
        specs[0] = pl.BlockSpec(memory_space=pltpu.SMEM)
    moved = sum(x.size * x.dtype.itemsize for x in list(operands) + list(outs))
    return pl.pallas_call(
        kernel,
        out_shape=outs,
        in_specs=specs,
        out_specs=[whole] * len(outs),
        scratch_shapes=scratch,
        compiler_params=pltpu.CompilerParams(vmem_limit_bytes=VMEM_BYTES),
        cost_estimate=pl.CostEstimate(flops=flops, bytes_accessed=moved, transcendentals=0),
        name=name,
    )(*operands)


def on_device(projected, short_filter, decay_rate, residue, skip, state_in, out_weight, cotangent):
    tokens, streams, width = projected.shape
    modes = decay_rate.shape[0]
    taps = short_filter.shape[1]
    rim = taps - 1
    rows = width // LANES
    count = lax.axis_size("ctx")
    dims = (tokens, rows, modes, streams, taps)
    shape = jax.ShapeDtypeStruct
    position = lax.axis_index("ctx").astype(jnp.int32).reshape(1)

    before = shifted(projected[tokens - rim :], "ctx", 1)
    after = shifted(projected[:rim], "ctx", -1)
    gathered = lax.all_gather(cotangent, "ch", axis=1, tiled=True)

    params = jnp.concatenate(
        [short_filter.reshape(streams * taps, width), decay_rate, residue, state_in, skip[None]], 0
    ).reshape(-1, rows, LANES)
    spare = -(tokens + 2 * rim) % SUB
    ext = jnp.concatenate(
        [before, projected, after, jnp.zeros((spare, streams, width), BF16)], 0
    )
    ext = jnp.transpose(ext, (1, 0, 2)).astype(F32)
    ext_tokens = ext.shape[1]

    tiles, total = call(
        functools.partial(total_kernel, dims),
        [shape((streams, ext_tokens * rows, LANES), F32), shape((modes, rows, LANES), BF16)],
        [pltpu.VMEM((modes, rows, LANES), F32)],
        "local_state",
        [ext, params],
        flops=2 * tokens * modes * width,
    )
    totals = lax.all_gather(total, "ctx", axis=0)
    gated, combined = call(
        functools.partial(forward_kernel, dims, count),
        [shape((tokens, width), BF16), shape(((tokens + rim) * rows, LANES), F32)],
        [pltpu.VMEM((tokens * rows, LANES), F32)],
        "forward_scan",
        [position, tiles, params, totals],
        scalar=True,
        flops=4 * tokens * modes * width,
    )
    piece = lax.all_gather(gated, "ctx", axis=0, tiled=True)
    partial_out = jnp.dot(gated, out_weight, preferred_element_type=F32)
    mixed_out = lax.psum_scatter(partial_out.astype(BF16), "ch", scatter_dimension=1, tiled=True)

    grad_gated = lax.dot_general(
        gathered, out_weight, (((1,), (1,)), ((), ())), preferred_element_type=F32
    )
    columns = lax.all_to_all(gathered, "ctx", split_axis=1, concat_axis=0, tiled=True)
    grad_tiles, first = call(
        functools.partial(first_kernel, dims),
        [shape((tokens * rows, LANES), F32), shape((modes + rim, rows, LANES), BF16)],
        [pltpu.VMEM((modes + rim, rows, LANES), F32)],
        "local_adjoint",
        [grad_gated, tiles, params],
        flops=2 * tokens * modes * width,
    )
    firsts = lax.all_gather(first, "ctx", axis=0)
    sum_rows = modes + streams * taps + 1
    stream_grads, sums, finals = call(
        functools.partial(backward_kernel, dims, count),
        [
            shape((streams, tokens, width), BF16),
            shape((sum_rows, rows, LANES), BF16),
            shape((2 * modes, rows, LANES), F32),
        ],
        [
            pltpu.VMEM((streams, (tokens + rim) * rows, LANES), F32),
            pltpu.VMEM((sum_rows, rows, LANES), F32),
        ],
        "backward_scan",
        [position, tiles, params, combined, grad_tiles, firsts],
        scalar=True,
        flops=8 * tokens * modes * width,
    )
    all_sums = lax.all_gather(sums, "ctx", axis=0)
    grad_weight = lax.dot_general(
        columns, piece, (((0,), (0,)), ((), ())), preferred_element_type=F32
    ).astype(BF16)
    grad_projected = jnp.transpose(stream_grads, (1, 0, 2))
    added = jnp.sum(all_sums.astype(F32), 0)
    grad_state = finals[:modes].reshape(modes, width)
    grad_residue = (added[:modes] + finals[modes:]).reshape(modes, width)
    grad_filter = added[modes : modes + streams * taps].reshape(streams, taps, width)
    grad_skip = added[-1].reshape(width)
    return (
        mixed_out,
        grad_projected,
        grad_weight,
        grad_filter,
        grad_residue,
        grad_skip,
        grad_state,
    )


def solution(mesh):
    in_specs = (
        P("ctx", None, "ch"),
        P(None, None, "ch"),
        P(None, "ch"),
        P(None, "ch"),
        P("ch"),
        P(None, "ch"),
        P("ch", None),
        P("ctx", "ch"),
    )
    out_specs = (
        P("ctx", "ch"),
        P("ctx", None, "ch"),
        P("ctx", "ch"),
        P(None, None, "ch"),
        P(None, "ch"),
        P("ch"),
        P(None, "ch"),
    )
    return jax.shard_map(
        on_device, mesh=mesh, in_specs=in_specs, out_specs=out_specs, check_vma=False
    )
```

time: 1220 us -> 165 us (0.14); the launches traced: 1200 us -> 164 us
  matrix products: 492 us -> 41.9 us
  other arithmetic: 291 us -> 1.67 us
  local copies, waits for them, and re-layouts: 236 us -> 22 us
  waiting for transfers between devices: 66.5 us -> 11.7 us
  starting transfers between devices: 56.8 us -> 8.14 us
  Pallas kernels: 0 us -> 19.4 us
    dot_general x10 -> x2, matrix products: 473 us -> 25.2 us  [the longest x1 16.7 us: on_device(): partial_out = jnp.dot(gated, out_weight, preferred_element_type=F32)]
    reduce_sum x19 -> x1, other arithmetic: 251 us -> 0.11 us  [on_device(): added = jnp.sum(all_sums.astype(F32), 0)]
    gather x2 -> x0, local copies, waits for them, and re-layouts: 82.7 us -> none  [on_device(): jnp.take(kernel, jnp.maximum(difference, 0), axis=0)]
    unnamed x94 -> x27, local copies, waits for them, and re-layouts: 73.9 us -> 15.1 us
    all_gather x0 -> x3, blocking collectives: none -> 45.6 us  [the longest x1 21.5 us: on_device(): firsts = lax.all_gather(first, 'ctx', axis=0)]
    ppermute x16 -> x2, waiting for transfers between devices: 42.9 us -> 0.01 us  [shifted(): return lax.ppermute(block, axis, route)]
    psum x1 -> x0, blocking collectives: 39.8 us -> none  [on_device(): lax.psum(filter_part.astype(jnp.bfloat16), 'ctx').astype(jnp.float32)]
    ppermute x16 -> x2, starting transfers between devices: 43.3 us -> 3.65 us  [shifted(): return lax.ppermute(block, axis, route)]
  transfers between devices with their start and end apart: 21 -> 6, of which waited for: 16 -> 1; matrix products, arithmetic and copies ran while one was open for 30% -> 36% of each run, Pallas kernels for 0% -> 12%
where the time goes in v1:
time: 165 us; the launch traced here: 164 us
  blocking collectives  45.6 us (28%)
  matrix products  41.9 us (25%)
  local copies, waits for them, and re-layouts  22 us (13%)
  Pallas kernels  19.4 us (12%)
  between operations  14 us (8%)
  waiting for transfers between devices  11.7 us (7%)
  starting transfers between devices  8.14 us (5%)
  other arithmetic  1.67 us (1%)
    all_gather x1, blocking collectives, on_device(): firsts = lax.all_gather(first, 'ctx', axis=0)  21.5 us
    pallas_call x4, Pallas kernels, call(): pl.pallas_call(kernel, out_shape=outs, in_specs=specs, out_specs=[whole]...  19.4 us
    dot_general x1, matrix products, on_device(): partial_out = jnp.dot(gated, out_weight, preferred_element_type=F32)  16.7 us
    dot_general x1, matrix products, on_device(): lax.dot_general(gathered, out_weight, (((1,), (1,)), ((), ())), preferred...  16.7 us
    unnamed x27, local copies, waits for them, and re-layouts  15.1 us
    all_gather x1, blocking collectives, on_device(): totals = lax.all_gather(total, 'ctx', axis=0)  14.1 us
    reduce_scatter x1, waiting for transfers between devices, on_device(): lax.psum_scatter(partial_out.astype(BF16), 'ch', scatter_dimension=1, til...  11.6 us
    all_gather x1, blocking collectives, on_device(): all_sums = lax.all_gather(sums, 'ctx', axis=0)  10 us
  transfers between devices with their start and end apart: 6, of which 1 were waited for; matrix products, arithmetic and copies ran while one was open for 36% of the time, Pallas kernels for 12%

profile of v1, /device:TPU:0, one launch (start us, length us, event | category | flops | bytes accessed | tf_op | source)
XLA Modules:
  0.0 164.3 jit_solution(4074971150835469952)
XLA Ops:
  7.2 2.2 %copy.20 = bf16[128,2048]{0,1:T(8,128)(2,1)} copy(bf16[128,2048]{1,0:T(8,128)(2,1)} %param.15) | data formatting | bytes 1048576 | tf_op args[7]
  9.5 1.0 fusion
  10.4 2.4 %collective-permute-start = (bf16[2,3,2048]{2,0,1:T(2,128)(2,1)S(1)}, bf16[2,3,2048]{2,0,1:T(2,128)(2,1)S(1)}, u32[]{:S(2)}, u32[]{:S(2)}) collective-permute-start(bf16[2,3,2048]{2,0,1:T(2,128)(2,1)S(1)} %get-tuple-element.53), channel_id=1, source_target_pairs={{0,4},{4,8},{8,12},{12,16},{16,20},{20,24},{24,28},{1,5},{5,9},{9,... | collective-permute-start | bytes 73736 | tf_op jit(solution)/shard_map/ppermute | solution.py:21
  12.8 1.3 collective-permute-start.1
  14.1 0.9 concatenate.18
  15.1 0.9 copy.23
  16.0 0.9 copy.24
  16.9 0.9 copy.25
  19.8 3.0 %local_state.1 = (f32[3,2176,128]{2,1,0:T(8,128)S(1)}, bf16[16,16,128]{2,1,0:T(8,128)(2,1)S(1)}) custom-call(f32[3,136,2048]{2,1,0:T(8,128)S(1)} %convert_bitcast_fusion.1.ext_ref, f32[58,16,128]{2,1,0:T(8,128)S(1)} %copy-done.1), custom_call_target="tpu_custom_call" | custom-call | flops 8388608 | bytes 7225344 | tf_op jit(solution)/shard_map/local_state/pallas_call | solution.py:336
  22.8 14.1 %all-gather = bf16[128,16,128]{2,1,0:T(8,128)(2,1)S(1)} all-gather(bf16[16,16,128]{2,1,0:T(8,128)(2,1)S(1)} %get-tuple-element.17), channel_id=2, replica_groups=mesh['ctx'=8,'ch'=4] {'ctx'}, dimensions={0}, use_global_device_ids=true | all-gather | bytes 589824 | tf_op jit(solution)/shard_map/all_gather | solution.py:381
  36.9 4.3 %forward_scan.1 = (bf16[128,2048]{1,0:T(8,128)(2,1)S(1)}, f32[2080,128]{1,0:T(8,128)S(1)}) custom-call(s32[1]{0:T(128)} %bitcast.pos_ref, f32[3,2176,128]{2,1,0:T(8,128)S(1)} %get-tuple-element.16.tiles_ref, f32[58,16,128]{2,1,0:T(8,128)S(1)} %copy-done.1, bf16[8,16,16,128]{3,2,1,0:T(8,128)(2,1)S(1)} %bitcast.36), custom_call_target="tpu_custom_call" | custom-call | flops 16777216 | bytes 5931012 | tf_op jit(solution)/shard_map/forward_scan/pallas_call | solution.py:336
  42.1 1.0 copy-done.4
  43.1 16.7 %convolution_convert_fusion = bf16[128,8192]{1,0:T(8,128)(2,1)} fusion(bf16[128,2048]{1,0:T(8,128)(2,1)} %copy-done.3, bf16[2048,8192]{1,0:T(8,128)(2,1)} %param.14), kind=kOutput, calls=%fused_computation | convolution fusion | flops 4296015872 | bytes 36175872 | tf_op jit(solution)/shard_map/dot_general | solution.py:392
  59.9 4.4 %all-to-all-start = ((bf16[128,8,1024]{0,2,1:T(8,128)(2,1)}), bf16[128,8,1024]{0,2,1:T(8,128)(2,1)}, u32[]{:S(2)}, u32[]{:S(2)}) async-start(bf16[128,8,1024]{0,2,1:T(8,128)(2,1)} %bitcast.37), calls=%async_computation.1 | async-start | bytes 4194304 | tf_op jit(solution)/shard_map/all_to_all | solution.py:398
  64.3 16.7 %fusion.2.grad_ref = f32[128,2048]{1,0:T(8,128)S(1)} fusion(bf16[128,8192]{0,1:T(8,128)(2,1)} %all-gather.6.cloned.1.call-done, bf16[2048,8192]{1,0:T(8,128)(2,1)} %param.14), kind=kOutput, calls=%fused_computation.15 | convolution fusion | flops 4294967296 | bytes 36700160 | tf_op jit(solution)/shard_map/dot_general | solution.py:395
  81.0 2.1 %local_adjoint.1 = (f32[2048,128]{1,0:T(8,128)S(1)}, bf16[18,16,128]{2,1,0:T(8,128)(2,1)S(1)}) custom-call(f32[128,2048]{1,0:T(8,128)S(1)} %fusion.2.grad_ref, f32[3,2176,128]{2,1,0:T(8,128)S(1)} %get-tuple-element.16.tiles_ref, f32[58,16,128]{2,1,0:T(8,128)S(1)} %copy-done.2), custom_call_target="tpu_custom_call" | custom-call | flops 8388608 | bytes 5988352 | tf_op jit(solution)/shard_map/local_adjoint/pallas_call | solution.py:336
  83.1 21.5 %all-gather.1 = bf16[144,16,128]{2,1,0:T(8,128)(2,1)S(1)} all-gather(bf16[18,16,128]{2,1,0:T(8,128)(2,1)S(1)} %get-tuple-element.21), channel_id=3, replica_groups=mesh['ctx'=8,'ch'=4] {'ctx'}, dimensions={0}, use_global_device_ids=true | all-gather | bytes 663552 | tf_op jit(solution)/shard_map/all_gather | solution.py:407
  104.6 9.9 %backward_scan.1 = (bf16[3,128,2048]{2,1,0:T(8,128)(2,1)}, bf16[26,16,128]{2,1,0:T(8,128)(2,1)S(1)}, f32[32,16,128]{2,1,0:T(8,128)S(1)}) custom-call(s32[1]{0:T(128)} %bitcast.pos_ref, f32[3,2176,128]{2,1,0:T(8,128)S(1)} %get-tuple-element.16.tiles_ref, f32[58,16,128]{2,1,0:T(8,128)S(1)} %copy-done.2, f32[2080,128]{1,0:T(8,128)S(1)} %copy-done.5, ...), custom_call_target="tpu_custom_call" | custom-call | flops 33554432 | bytes 8462340 | tf_op jit(solution)/shard_map/backward_scan/pallas_call | solution.py:336
  115.2 10.0 %all-gather.2 = bf16[208,16,128]{2,1,0:T(8,128)(2,1)S(1)} all-gather(bf16[26,16,128]{2,1,0:T(8,128)(2,1)S(1)} %get-tuple-element.23), channel_id=4, replica_groups=mesh['ctx'=8,'ch'=4] {'ctx'}, dimensions={0}, use_global_device_ids=true | all-gather | bytes 958464 | tf_op jit(solution)/shard_map/all_gather | solution.py:425
  126.6 1.0 fusion.1
  128.4 2.9 %copy.21 = bf16[8,128,1024]{2,1,0:T(8,128)(2,1)S(1)} copy(bf16[8,128,1024]{1,2,0:T(8,128)(2,1)} %bitcast.7) | data formatting | bytes 4194304 | tf_op jit(solution)/shard_map/all_to_all | solution.py:398
  131.3 8.5 %convert_bitcast_fusion = bf16[1024,2048]{0,1:T(8,128)(2,1)} fusion(bf16[1024,2048]{1,0:T(8,128)(2,1)} %all-gather.8.cloned.1.call-done, bf16[1024,1024]{1,0:T(8,128)(2,1)S(1)} %bitcast.39), kind=kOutput, calls=%fused_computation.1 | convolution fusion | flops 4297064448 | bytes 10485760 | tf_op jit(solution)/shard_map/dot_general | solution.py:426
  139.8 6.4 %copy.22 = bf16[1024,2048]{1,0:T(8,128)(2,1)} copy(bf16[1024,2048]{0,1:T(8,128)(2,1)} %convert_bitcast_fusion) | data formatting | bytes 8388608
  146.2 11.6 %reduce-scatter.2.cloned.1.call-done = bf16[128,2048]{1,0:T(8,128)(2,1)} async-done(((bf16[128,8192]{1,0:T(8,128)(2,1)}), bf16[128,2048]{1,0:T(8,128)(2,1)}) %reduce-scatter.2.cloned.1.call-update) | async-done | bytes 524304 | tf_op jit(solution)/shard_map/reduce_scatter | solution.py:393
  (41 shorter events, 5.7 us)
Async XLA Ops:
  7.2 11.7 %copy-start.7 = (bf16[128,3,2048]{2,0,1:T(8,128)(2,1)S(1)}, bf16[128,3,2048]{2,0,1:T(8,128)(2,1)}, u32[]{:S(2)}) copy-start(bf16[128,3,2048]{2,0,1:T(8,128)(2,1)} %param.8) | copy-start | bytes 4718596
  7.2 10.8 %copy-start.8 = (f32[2048]{0:T(1024)S(1)}, f32[2048]{0:T(1024)}, u32[]{:S(2)}) copy-start(f32[2048]{0:T(1024)} %param.12) | copy-start | bytes 24580
  7.2 52.7 %all-gather.6.cloned.1.call-start = ((), (), s32[]{:S(2)}) async-start(), calls=%async_computation.3 | async-start | bytes 2621440 | tf_op jit(solution)/shard_map/all_gather | solution.py:361
  9.4 121.9 %all-gather.8.cloned.1.call-start = ((), (), s32[]{:S(2)}) async-start(), calls=%async_computation.4 | async-start | bytes 4718592 | tf_op jit(solution)/shard_map/all_gather | solution.py:391
  10.4 8.4 %collective-permute-start = (bf16[2,3,2048]{2,0,1:T(2,128)(2,1)S(1)}, bf16[2,3,2048]{2,0,1:T(2,128)(2,1)S(1)}, u32[]{:S(2)}, u32[]{:S(2)}) collective-permute-start(bf16[2,3,2048]{2,0,1:T(2,128)(2,1)S(1)} %get-tuple-element.53), channel_id=1, source_target_pairs={{0,4},{4,8},{8,12},{12,16},{16,20},{20,24},{24,28},{1,5},{5,9},{9,... | collective-permute-start | bytes 73736 | tf_op jit(solution)/shard_map/ppermute | solution.py:21
  12.8 6.0 %collective-permute-start.1 = (bf16[2,3,2048]{2,0,1:T(2,128)(2,1)S(1)}, bf16[2,3,2048]{2,0,1:T(2,128)(2,1)S(1)}, u32[]{:S(2)}, u32[]{:S(2)}) collective-permute-start(bf16[2,3,2048]{2,0,1:T(2,128)(2,1)S(1)} %get-tuple-element.54), channel_id=1, source_target_pairs={{4,0},{8,4},{12,8},{16,12},{20,16},{24,20},{28,24},{5,1},{9,5},{13... | collective-permute-start | bytes 73736 | tf_op jit(solution)/shard_map/ppermute | solution.py:21
  18.0 0.8 copy-start
  18.7 1.1 copy-start.1
  41.3 0.8 copy-start.3
  42.1 1.0 copy-start.4
  43.1 114.8 %reduce-scatter.2.cloned.1.call-start = ((), (), s32[]{:S(2)}) async-start(), calls=%async_computation.2 | async-start | bytes 2621440 | tf_op jit(solution)/shard_map/reduce_scatter | solution.py:393
  59.9 68.5 %all-to-all-start = ((bf16[128,8,1024]{0,2,1:T(8,128)(2,1)}), bf16[128,8,1024]{0,2,1:T(8,128)(2,1)}, u32[]{:S(2)}, u32[]{:S(2)}) async-start(bf16[128,8,1024]{0,2,1:T(8,128)(2,1)} %bitcast.37), calls=%async_computation.1 | async-start | bytes 4194304 | tf_op jit(solution)/shard_map/all_to_all | solution.py:398
  64.2 16.7 %copy-start.2 = (f32[58,16,128]{2,1,0:T(8,128)S(1)}, f32[58,16,128]{2,1,0:T(8,128)}, u32[]{:S(2)}) copy-start(f32[58,16,128]{2,1,0:T(8,128)} %copy-done) | copy-start | bytes 1425412
  81.0 23.6 %copy-start.5 = (f32[2080,128]{1,0:T(8,128)S(1)}, f32[2080,128]{1,0:T(8,128)}, u32[]{:S(2)}) copy-start(f32[2080,128]{1,0:T(8,128)} %copy-done.4) | copy-start | bytes 3194884
  114.5 0.7 copy-start.6
Sparse Core Ops, SparseCore 0:
  9.6 48.6 all-gather.5
  60.7 50.1 all-gather.7
  113.8 43.9 reduce-scatter.1

commit v2 on v1

--- a/solution.py
+++ b/solution.py
@@ -327,6 +327,113 @@
     sums_ref[...] = sums[...].astype(BF16)
 
 
+def gather_kernel(count, block_ref, out_ref, send_sems, recv_sems):
+    me = lax.axis_index("ctx")
+    barrier = pltpu.get_barrier_semaphore()
+    for step in range(1, count):
+        pl.semaphore_signal(
+            barrier,
+            inc=1,
+            device_id={"ctx": lax.rem(me + step, count)},
+            device_id_type=pl.DeviceIdType.MESH,
+        )
+    pl.semaphore_wait(barrier, count - 1)
+    copies = []
+    for step in range(1, count):
+        copy = pltpu.make_async_remote_copy(
+            src_ref=block_ref,
+            dst_ref=out_ref.at[me],
+            send_sem=send_sems.at[step - 1],
+            recv_sem=recv_sems.at[step - 1],
+            device_id={"ctx": lax.rem(me + step, count)},
+            device_id_type=pl.DeviceIdType.MESH,
+        )
+        copy.start()
+        copies.append(copy)
+    out_ref[me] = block_ref[...]
+    for copy in copies:
+        copy.wait()
+
+
+def gather_small(block, name, collective_id):
+    count = lax.axis_size("ctx")
+    whole = pl.BlockSpec(memory_space=pltpu.VMEM)
+    return pl.pallas_call(
+        functools.partial(gather_kernel, count),
+        out_shape=jax.ShapeDtypeStruct((count,) + block.shape, block.dtype),
+        in_specs=[whole],
+        out_specs=whole,
+        scratch_shapes=[pltpu.SemaphoreType.DMA((count - 1,))] * 2,
+        compiler_params=pltpu.CompilerParams(
+            collective_id=collective_id, has_side_effects=True, vmem_limit_bytes=VMEM_BYTES
+        ),
+        cost_estimate=pl.CostEstimate(
+            flops=0, bytes_accessed=2 * count * block.size * 2, transcendentals=0
+        ),
+        name=name,
+    )(block)
+
+
+def exchanged_blocks(block, partial_out):
+    count = lax.axis_size("ctx")
+
+    def swap(value, k):
+        return lax.ppermute(value, "ctx", [(i, i ^ k) for i in range(count)])
+
+    blocks = {0: block}
+    for k in range(2, count, 2):
+        blocks[k] = swap(block, k)
+    blocks[1] = swap(block, 1)
+    firsts, partial_out = lax.optimization_barrier(
+        ([blocks[k] for k in range(2, count, 2)], partial_out)
+    )
+    for k, value in zip(range(2, count, 2), firsts):
+        blocks[k] = value
+        blocks[k + 1] = swap(value, 1)
+    return [blocks[k] for k in range(count)], partial_out
+
+
+def weight_kernel(count, pos_ref, columns_ref, *refs):
+    blocks, out_ref, ordered = refs[:count], refs[count], refs[count + 1]
+    tokens = blocks[0].shape[0]
+
+    @pl.when(pl.program_id(0) == 0)
+    def _():
+        for k in range(count):
+            owner = jnp.bitwise_xor(pos_ref[0], k)
+            ordered[pl.ds(pl.multiple_of(owner * tokens, tokens), tokens), :] = blocks[k][...]
+
+    out_ref[...] = lax.dot_general(
+        columns_ref[...], ordered[...], (((0,), (0,)), ((), ())), preferred_element_type=F32
+    ).astype(BF16)
+
+
+def weight_grad(position, columns, blocks):
+    count = len(blocks)
+    total, features = columns.shape
+    width = blocks[0].shape[1]
+    step = min(256, features)
+    return pl.pallas_call(
+        functools.partial(weight_kernel, count),
+        grid=(features // step,),
+        out_shape=jax.ShapeDtypeStruct((features, width), BF16),
+        in_specs=[
+            pl.BlockSpec(memory_space=pltpu.SMEM),
+            pl.BlockSpec((total, step), lambda i: (0, i)),
+        ]
+        + [pl.BlockSpec(block.shape, lambda i: (0, 0)) for block in blocks],
+        out_specs=pl.BlockSpec((step, width), lambda i: (i, 0)),
+        scratch_shapes=[pltpu.VMEM((total, width), BF16)],
+        compiler_params=pltpu.CompilerParams(vmem_limit_bytes=VMEM_BYTES),
+        cost_estimate=pl.CostEstimate(
+            flops=2 * total * features * width,
+            bytes_accessed=2 * (total * features + total * width + features * width),
+            transcendentals=0,
+        ),
+        name="weight_grad",
+    )(position, columns, *blocks)
+
+
 def call(kernel, outs, scratch, name, operands, scalar=False, flops=0):
     whole = pl.BlockSpec(memory_space=pltpu.VMEM)
     specs = [whole] * len(operands)
@@ -378,7 +485,7 @@
         [ext, params],
         flops=2 * tokens * modes * width,
     )
-    totals = lax.all_gather(total, "ctx", axis=0)
+    totals = gather_small(total, "gather_states", 0)
     gated, combined = call(
         functools.partial(forward_kernel, dims, count),
         [shape((tokens, width), BF16), shape(((tokens + rim) * rows, LANES), F32)],
@@ -388,9 +495,9 @@
         scalar=True,
         flops=4 * tokens * modes * width,
     )
-    piece = lax.all_gather(gated, "ctx", axis=0, tiled=True)
-    partial_out = jnp.dot(gated, out_weight, preferred_element_type=F32)
-    mixed_out = lax.psum_scatter(partial_out.astype(BF16), "ch", scatter_dimension=1, tiled=True)
+    partial_out = jnp.dot(gated, out_weight, preferred_element_type=F32).astype(BF16)
+    blocks, partial_out = exchanged_blocks(gated, partial_out)
+    mixed_out = lax.psum_scatter(partial_out, "ch", scatter_dimension=1, tiled=True)
 
     grad_gated = lax.dot_general(
         gathered, out_weight, (((1,), (1,)), ((), ())), preferred_element_type=F32
@@ -404,7 +511,7 @@
         [grad_gated, tiles, params],
         flops=2 * tokens * modes * width,
     )
-    firsts = lax.all_gather(first, "ctx", axis=0)
+    firsts = gather_small(first, "gather_adjoints", 1)
     sum_rows = modes + streams * taps + 1
     stream_grads, sums, finals = call(
         functools.partial(backward_kernel, dims, count),
@@ -422,10 +529,8 @@
         scalar=True,
         flops=8 * tokens * modes * width,
     )
-    all_sums = lax.all_gather(sums, "ctx", axis=0)
-    grad_weight = lax.dot_general(
-        columns, piece, (((0,), (0,)), ((), ())), preferred_element_type=F32
-    ).astype(BF16)
+    all_sums = gather_small(sums, "gather_sums", 2)
+    grad_weight = weight_grad(position, columns, blocks)
     grad_projected = jnp.transpose(stream_grads, (1, 0, 2))
     added = jnp.sum(all_sums.astype(F32), 0)
     grad_state = finals[:modes].reshape(modes, width)

time: 165 us -> 150 us (0.909)
  Pallas kernels: 19.4 us -> 66.9 us
  blocking collectives: 45.6 us -> 0 us
  local copies, waits for them, and re-layouts: 22 us -> 12.9 us
  matrix products: 41.9 us -> 33 us
  starting transfers between devices: 8.14 us -> 12.9 us
  waiting for transfers between devices: 11.7 us -> 7.85 us
    pallas_call x0 -> x4, Pallas kernels: none -> 46.8 us  [the longest x3 37.8 us: gather_small(): pl.pallas_call(functools.partial(gather_kernel, count), out_shape=jax.Sha...]
    all_gather x3 -> x0, blocking collectives: 45.6 us -> none  [the longest x1 21.5 us: on_device(): firsts = lax.all_gather(first, 'ctx', axis=0)]
    reduce_scatter x1, waiting for transfers between devices: 11.6 us -> 0.01 us  [on_device(): lax.psum_scatter(partial_out, 'ch', scatter_dimension=1, tiled=True)]
    unnamed x27 -> x19, local copies, waits for them, and re-layouts: 15.1 us -> 5.01 us
    dot_general x2 -> x1, matrix products: 25.2 us -> 16.6 us  [on_device(): jnp.dot(gated, out_weight, preferred_element_type=F32).astype(BF16)]
    ppermute x0 -> x7, waiting for transfers between devices: none -> 7.14 us  [swap(): return lax.ppermute(value, 'ctx', [(i, i ^ k) for i in range(count)])]
    ppermute x0 -> x7, starting transfers between devices: none -> 4.57 us  [swap(): return lax.ppermute(value, 'ctx', [(i, i ^ k) for i in range(count)])]
  transfers between devices with their start and end apart: 6 -> 12, of which waited for: 1 -> 1; matrix products, arithmetic and copies ran while one was open for 36% -> 30% of each run, Pallas kernels for 12% -> 45%
where the time goes in v2:
time: 150 us; the launch traced here: 149 us
  Pallas kernels  66.9 us (45%)
  matrix products  33 us (22%)
  between operations  14.2 us (9%)
  local copies, waits for them, and re-layouts  12.9 us (9%)
  starting transfers between devices  12.9 us (9%)
  waiting for transfers between devices  7.85 us (5%)
    pallas_call x3, Pallas kernels, gather_small(): pl.pallas_call(functools.partial(gather_kernel, count), out_shape=jax.Sha...  37.8 us
    pallas_call x4, Pallas kernels, call(): pl.pallas_call(kernel, out_shape=outs, in_specs=specs, out_specs=[whole]...  20.2 us
    dot_general x1, matrix products, on_device(): jnp.dot(gated, out_weight, preferred_element_type=F32).astype(BF16)  16.6 us
    dot_general x1, matrix products, on_device(): lax.dot_general(gathered, out_weight, (((1,), (1,)), ((), ())), preferred...  16.4 us
    pallas_call x1, Pallas kernels, weight_grad(): pl.pallas_call(functools.partial(weight_kernel, count), grid=(features //...  8.93 us
    ppermute x7, waiting for transfers between devices, swap(): return lax.ppermute(value, 'ctx', [(i, i ^ k) for i in range(count)])  7.14 us
    unnamed x19, local copies, waits for them, and re-layouts  5.01 us
    all_to_all x1, starting transfers between devices, on_device(): lax.all_to_all(gathered, 'ctx', split_axis=1, concat_axis=0, tiled=True)  4.58 us
  transfers between devices with their start and end apart: 12, of which 1 were waited for; matrix products, arithmetic and copies ran while one was open for 30% of the time, Pallas kernels for 45%

profile of v2, /device:TPU:0, one launch (start us, length us, event | category | flops | bytes accessed | tf_op | source)
XLA Modules:
  0.0 148.5 jit_solution(4139560852178429003)
XLA Ops:
  8.0 1.0 fusion
  8.9 2.4 %collective-permute-start = (bf16[2,3,2048]{2,0,1:T(2,128)(2,1)S(1)}, bf16[2,3,2048]{2,0,1:T(2,128)(2,1)S(1)}, u32[]{:S(2)}, u32[]{:S(2)}) collective-permute-start(bf16[2,3,2048]{2,0,1:T(2,128)(2,1)S(1)} %get-tuple-element.33), channel_id=1, source_target_pairs={{0,4},{4,8},{8,12},{12,16},{16,20},{20,24},{24,28},{1,5},{5,9},{9,... | collective-permute-start | bytes 73736 | tf_op jit(solution)/shard_map/ppermute | solution.py:21
  11.3 1.3 collective-permute-start.1
  12.6 0.9 concatenate.18
  13.6 0.9 copy.17
  14.5 0.9 copy.18
  15.4 0.9 copy.19
  17.1 0.8 copy-done
  19.0 3.0 %local_state.1 = (f32[3,2176,128]{2,1,0:T(8,128)S(1)}, bf16[16,16,128]{2,1,0:T(8,128)(2,1)S(1)}) custom-call(f32[3,136,2048]{2,1,0:T(8,128)S(1)} %convert_bitcast_fusion.ext_ref, f32[58,16,128]{2,1,0:T(8,128)S(1)} %copy-done.1), custom_call_target="tpu_custom_call" | custom-call | flops 8388608 | bytes 7225344 | tf_op jit(solution)/shard_map/local_state/pallas_call | solution.py:443
  22.0 13.2 %gather_states.1.totals_ref = bf16[8,16,16,128]{3,2,1,0:T(8,128)(2,1)S(1)} custom-call(bf16[16,16,128]{2,1,0:T(8,128)(2,1)S(1)} %get-tuple-element.21.block_ref), custom_call_target="tpu_custom_call" | custom-call | bytes 1048576 | tf_op jit(solution)/shard_map/gather_states/pallas_call | solution.py:361
  35.2 5.1 %forward_scan.1 = (bf16[128,2048]{1,0:T(8,128)(2,1)}, f32[2080,128]{1,0:T(8,128)S(1)}) custom-call(s32[1]{0:T(128)} %bitcast.pos_ref, f32[3,2176,128]{2,1,0:T(8,128)S(1)} %get-tuple-element.20.tiles_ref, f32[58,16,128]{2,1,0:T(8,128)S(1)} %copy-done.1, bf16[8,16,16,128]{3,2,1,0:T(8,128)(2,1)S(1)} %gather_states.1.totals_ref), custom_call_target="tpu_custom_call" | custom-call | flops 16777216 | bytes 5931012 | tf_op jit(solution)/shard_map/forward_scan/pallas_call | solution.py:443
  40.3 1.0 copy-done.3
  41.3 1.4 collective-permute-start.4
  43.3 1.5 %collective-permute-start.2 = (bf16[128,2048]{1,0:T(8,128)(2,1)}, bf16[128,2048]{1,0:T(8,128)(2,1)}, u32[]{:S(2)}, u32[]{:S(2)}) collective-permute-start(bf16[128,2048]{1,0:T(8,128)(2,1)} %get-tuple-element.22.refs_0_), channel_id=1, source_target_pairs={{0,8},{4,12},{8,0},{12,4},{16,24},{20,28},{24,16},{28,20},{1,9},{5... | collective-permute-start | bytes 1572872 | tf_op jit(solution)/shard_map/ppermute | solution.py:381
  44.8 16.6 %convolution_convert_fusion = bf16[128,8192]{1,0:T(8,128)(2,1)} fusion(bf16[128,2048]{1,0:T(8,128)(2,1)} %get-tuple-element.22.refs_0_, bf16[2048,8192]{1,0:T(8,128)(2,1)} %param.14), kind=kOutput, calls=%fused_computation | convolution fusion | flops 4296015872 | bytes 36175872 | tf_op jit(solution)/shard_map/dot_general | solution.py:498
  61.4 7.1 %collective-permute-done.3.refs_4_ = bf16[128,2048]{1,0:T(8,128)(2,1)} collective-permute-done((bf16[128,2048]{1,0:T(8,128)(2,1)}, bf16[128,2048]{1,0:T(8,128)(2,1)}, u32[]{:S(2)}, u32[]{:S(2)}) %collective-permute-start.3) | collective-permute-done | bytes 524320 | tf_op jit(solution)/shard_map/ppermute | solution.py:381
  69.6 3.1 %copy.25 = bf16[16,8,8,1024]{3,2,0,1:T(8,128)(2,1)} copy(bf16[16,8,8,1024]{3,2,1,0:T(8,128)(2,1)} %bitcast.31) | data formatting | bytes 4194304 | tf_op jit(solution)/shard_map/all_to_all | solution.py:505
  72.8 4.6 %all-to-all-start = ((bf16[128,8,1024]{2,0,1:T(8,128)(2,1)}), bf16[128,8,1024]{2,0,1:T(8,128)(2,1)}, u32[]{:S(2)}, u32[]{:S(2)}) async-start(bf16[128,8,1024]{2,0,1:T(8,128)(2,1)} %bitcast.32), calls=%async_computation.1 | async-start | bytes 4194304 | tf_op jit(solution)/shard_map/all_to_all | solution.py:505
  77.4 16.4 %fusion.2.grad_ref = f32[128,2048]{1,0:T(8,128)S(1)} fusion(bf16[128,8192]{1,0:T(8,128)(2,1)} %all-gather.2.cloned.1.call-done, bf16[2048,8192]{1,0:T(8,128)(2,1)} %param.14), kind=kOutput, calls=%fused_computation.15 | convolution fusion | flops 4294967296 | bytes 36700160 | tf_op jit(solution)/shard_map/dot_general | solution.py:502
  93.8 2.1 %local_adjoint.1 = (f32[2048,128]{1,0:T(8,128)S(1)}, bf16[18,16,128]{2,1,0:T(8,128)(2,1)S(1)}) custom-call(f32[128,2048]{1,0:T(8,128)S(1)} %fusion.2.grad_ref, f32[3,2176,128]{2,1,0:T(8,128)S(1)} %get-tuple-element.20.tiles_ref, f32[58,16,128]{2,1,0:T(8,128)S(1)} %copy-done.2), custom_call_target="tpu_custom_call" | custom-call | flops 8388608 | bytes 5988352 | tf_op jit(solution)/shard_map/local_adjoint/pallas_call | solution.py:443
  95.9 12.7 %gather_adjoints.1.firsts_ref = bf16[8,18,16,128]{3,2,1,0:T(8,128)(2,1)S(1)} custom-call(bf16[18,16,128]{2,1,0:T(8,128)(2,1)S(1)} %get-tuple-element.26.block_ref), custom_call_target="tpu_custom_call" | custom-call | bytes 1179648 | tf_op jit(solution)/shard_map/gather_adjoints/pallas_call | solution.py:361
  108.7 9.9 %backward_scan.1 = (bf16[3,128,2048]{2,1,0:T(8,128)(2,1)}, bf16[26,16,128]{2,1,0:T(8,128)(2,1)S(1)}, f32[32,16,128]{2,1,0:T(8,128)S(1)}) custom-call(s32[1]{0:T(128)} %bitcast.pos_ref, f32[3,2176,128]{2,1,0:T(8,128)S(1)} %get-tuple-element.20.tiles_ref, f32[58,16,128]{2,1,0:T(8,128)S(1)} %copy-done.2, f32[2080,128]{1,0:T(8,128)S(1)} %copy-done.4, ...), custom_call_target="tpu_custom_call" | custom-call | flops 33554432 | bytes 8462340 | tf_op jit(solution)/shard_map/backward_scan/pallas_call | solution.py:443
  118.6 11.9 %gather_sums.1 = bf16[8,26,16,128]{3,2,1,0:T(8,128)(2,1)S(1)} custom-call(bf16[26,16,128]{2,1,0:T(8,128)(2,1)S(1)} %get-tuple-element.31.block_ref), custom_call_target="tpu_custom_call" | custom-call | bytes 1703936 | tf_op jit(solution)/shard_map/gather_sums/pallas_call | solution.py:361
  132.8 8.9 %weight_grad.1 = bf16[1024,2048]{1,0:T(8,128)(2,1)} custom-call(s32[1]{0:T(128)} %bitcast.pos_ref, bf16[1024,1024]{1,0:T(8,128)(2,1)} %bitcast.5.columns_ref, bf16[128,2048]{1,0:T(8,128)(2,1)} %get-tuple-element.22.refs_0_, bf16[128,2048]{1,0:T(8,128)(2,1)} %collective-permute-done.5.refs_1_, bf16[128,2048]{1,0:T(8,128)(2,1)} %collective-permute-done.2.refs_2_, ...), custom_call_target="tpu_custom_call" | custom-call | flops 4294967296 | bytes 10485760 | tf_op jit(solution)/shard_map/weight_grad/pallas_call | solution.py:416
  (44 shorter events, 6.5 us)
Async XLA Ops:
  7.2 10.8 %copy-start.5 = (bf16[128,3,2048]{2,0,1:T(8,128)(2,1)S(1)}, bf16[128,3,2048]{2,0,1:T(8,128)(2,1)}, u32[]{:S(2)}) copy-start(bf16[128,3,2048]{2,0,1:T(8,128)(2,1)} %param.8) | copy-start | bytes 4718596
  7.2 62.5 %all-gather.2.cloned.1.call-start = ((), (), s32[]{:S(2)}) async-start(), calls=%async_computation.3 | async-start | bytes 2621440 | tf_op jit(solution)/shard_map/all_gather | solution.py:468
  7.9 133.8 %reduce-scatter.2.cloned.1.call-start = ((), (), s32[]{:S(2)}) async-start(), calls=%async_computation.2 | async-start | bytes 2621440 | tf_op jit(solution)/shard_map/reduce_scatter | solution.py:500
  8.9 9.1 %collective-permute-start = (bf16[2,3,2048]{2,0,1:T(2,128)(2,1)S(1)}, bf16[2,3,2048]{2,0,1:T(2,128)(2,1)S(1)}, u32[]{:S(2)}, u32[]{:S(2)}) collective-permute-start(bf16[2,3,2048]{2,0,1:T(2,128)(2,1)S(1)} %get-tuple-element.33), channel_id=1, source_target_pairs={{0,4},{4,8},{8,12},{12,16},{16,20},{20,24},{24,28},{1,5},{5,9},{9,... | collective-permute-start | bytes 73736 | tf_op jit(solution)/shard_map/ppermute | solution.py:21
  11.3 6.7 %collective-permute-start.1 = (bf16[2,3,2048]{2,0,1:T(2,128)(2,1)S(1)}, bf16[2,3,2048]{2,0,1:T(2,128)(2,1)S(1)}, u32[]{:S(2)}, u32[]{:S(2)}) collective-permute-start(bf16[2,3,2048]{2,0,1:T(2,128)(2,1)S(1)} %get-tuple-element.34), channel_id=1, source_target_pairs={{4,0},{8,4},{12,8},{16,12},{20,16},{24,20},{28,24},{5,1},{9,5},{13... | collective-permute-start | bytes 73736 | tf_op jit(solution)/shard_map/ppermute | solution.py:21
  17.1 0.8 copy-start
  17.9 1.1 copy-start.1
  40.3 1.0 copy-start.3
  41.3 20.1 %collective-permute-start.4 = (bf16[128,2048]{1,0:T(8,128)(2,1)}, bf16[128,2048]{1,0:T(8,128)(2,1)}, u32[]{:S(2)}, u32[]{:S(2)}) collective-permute-start(bf16[128,2048]{1,0:T(8,128)(2,1)} %get-tuple-element.22.refs_0_), channel_id=1, source_target_pairs={{0,24},{4,28},{8,16},{12,20},{16,8},{20,12},{24,0},{28,4},{1,25},{... | collective-permute-start | bytes 1572872 | tf_op jit(solution)/shard_map/ppermute | solution.py:381
  42.7 25.8 %collective-permute-start.3 = (bf16[128,2048]{1,0:T(8,128)(2,1)}, bf16[128,2048]{1,0:T(8,128)(2,1)}, u32[]{:S(2)}, u32[]{:S(2)}) collective-permute-start(bf16[128,2048]{1,0:T(8,128)(2,1)} %get-tuple-element.22.refs_0_), channel_id=1, source_target_pairs={{0,16},{4,20},{8,24},{12,28},{16,0},{20,4},{24,8},{28,12},{1,17},{... | collective-permute-start | bytes 1572872 | tf_op jit(solution)/shard_map/ppermute | solution.py:381
  43.3 25.3 %collective-permute-start.2 = (bf16[128,2048]{1,0:T(8,128)(2,1)}, bf16[128,2048]{1,0:T(8,128)(2,1)}, u32[]{:S(2)}, u32[]{:S(2)}) collective-permute-start(bf16[128,2048]{1,0:T(8,128)(2,1)} %get-tuple-element.22.refs_0_), channel_id=1, source_target_pairs={{0,8},{4,12},{8,0},{12,4},{16,24},{20,28},{24,16},{28,20},{1,9},{5... | collective-permute-start | bytes 1572872 | tf_op jit(solution)/shard_map/ppermute | solution.py:381
  68.6 64.2 %collective-permute-start.5 = (bf16[128,2048]{1,0:T(8,128)(2,1)}, bf16[128,2048]{1,0:T(8,128)(2,1)}, u32[]{:S(2)}, u32[]{:S(2)}) collective-permute-start(bf16[128,2048]{1,0:T(8,128)(2,1)} %get-tuple-element.22.refs_0_), channel_id=1, source_target_pairs={{0,4},{4,0},{8,12},{12,8},{16,20},{20,16},{24,28},{28,24},{1,5},{5... | collective-permute-start | bytes 1572872 | tf_op jit(solution)/shard_map/ppermute | solution.py:381
  68.7 64.0 %collective-permute-start.6 = (bf16[128,2048]{1,0:T(8,128)(2,1)}, bf16[128,2048]{1,0:T(8,128)(2,1)}, u32[]{:S(2)}, u32[]{:S(2)}) collective-permute-start(bf16[128,2048]{1,0:T(8,128)(2,1)} %collective-permute-done.2.refs_2_), channel_id=1, source_target_pairs={{0,4},{4,0},{8,12},{12,8},{16,20},{20,16},{24,28},{28,24},{1,5},{5... | collective-permute-start | bytes 1572872 | tf_op jit(solution)/shard_map/ppermute | solution.py:381
  69.1 63.6 %collective-permute-start.7 = (bf16[128,2048]{1,0:T(8,128)(2,1)}, bf16[128,2048]{1,0:T(8,128)(2,1)}, u32[]{:S(2)}, u32[]{:S(2)}) collective-permute-start(bf16[128,2048]{1,0:T(8,128)(2,1)} %collective-permute-done.3.refs_4_), channel_id=1, source_target_pairs={{0,4},{4,0},{8,12},{12,8},{16,20},{20,16},{24,28},{28,24},{1,5},{5... | collective-permute-start | bytes 1572872 | tf_op jit(solution)/shard_map/ppermute | solution.py:381
  69.2 63.5 %collective-permute-start.8 = (bf16[128,2048]{1,0:T(8,128)(2,1)}, bf16[128,2048]{1,0:T(8,128)(2,1)}, u32[]{:S(2)}, u32[]{:S(2)}) collective-permute-start(bf16[128,2048]{1,0:T(8,128)(2,1)} %collective-permute-done.4.refs_6_), channel_id=1, source_target_pairs={{0,4},{4,0},{8,12},{12,8},{16,20},{20,16},{24,28},{28,24},{1,5},{5... | collective-permute-start | bytes 1572872 | tf_op jit(solution)/shard_map/ppermute | solution.py:381
  72.8 60.0 %all-to-all-start = ((bf16[128,8,1024]{2,0,1:T(8,128)(2,1)}), bf16[128,8,1024]{2,0,1:T(8,128)(2,1)}, u32[]{:S(2)}, u32[]{:S(2)}) async-start(bf16[128,8,1024]{2,0,1:T(8,128)(2,1)} %bitcast.32), calls=%async_computation.1 | async-start | bytes 4194304 | tf_op jit(solution)/shard_map/all_to_all | solution.py:505
  77.4 16.4 %copy-start.2 = (f32[58,16,128]{2,1,0:T(8,128)S(1)}, f32[58,16,128]{2,1,0:T(8,128)}, u32[]{:S(2)}) copy-start(f32[58,16,128]{2,1,0:T(8,128)} %copy-done) | copy-start | bytes 1425412
  93.8 14.9 %copy-start.4 = (f32[2080,128]{1,0:T(8,128)S(1)}, f32[2080,128]{1,0:T(8,128)}, u32[]{:S(2)}) copy-start(f32[2080,128]{1,0:T(8,128)} %copy-done.3) | copy-start | bytes 3194884
Sparse Core Ops, SparseCore 0:
  9.6 48.6 all-gather.1
  68.7 44.0 reduce-scatter.1

commit v3 on v2

--- a/solution.py
+++ b/solution.py
@@ -529,10 +529,12 @@
         scalar=True,
         flops=8 * tokens * modes * width,
     )
-    all_sums = gather_small(sums, "gather_sums", 2)
+    all_sums = [sums] + [
+        lax.ppermute(sums, "ctx", [(i, i ^ k) for i in range(count)]) for k in range(1, count)
+    ]
     grad_weight = weight_grad(position, columns, blocks)
     grad_projected = jnp.transpose(stream_grads, (1, 0, 2))
-    added = jnp.sum(all_sums.astype(F32), 0)
+    added = tree_sum([part_sums.astype(F32) for part_sums in all_sums])
     grad_state = finals[:modes].reshape(modes, width)
     grad_residue = (added[:modes] + finals[modes:]).reshape(modes, width)
     grad_filter = added[modes : modes + streams * taps].reshape(streams, taps, width)

time: 150 us -> 150 us (level)
  Pallas kernels: 66.9 us -> 54.3 us
  starting transfers between devices: 12.9 us -> 20.2 us
  waiting for transfers between devices: 7.85 us -> 14 us
    pallas_call x3 -> x2, Pallas kernels: 37.8 us -> 25.9 us  [gather_small(): pl.pallas_call(functools.partial(gather_kernel, count), out_shape=jax.Sha...]
    ppermute x0 -> x7, starting transfers between devices: none -> 7.79 us  [on_device(): lax.ppermute(sums, 'ctx', [(i, i ^ k) for i in range(count)])]
    ppermute x0 -> x7, waiting for transfers between devices: none -> 5.39 us  [on_device(): lax.ppermute(sums, 'ctx', [(i, i ^ k) for i in range(count)])]
  transfers between devices with their start and end apart: 12 -> 19, of which waited for: 1 -> 5; matrix products, arithmetic and copies ran while one was open for 30% -> 30% of each run, Pallas kernels for 45% -> 36%
where the time goes in v3:
time: 150 us; the launch traced here: 149 us
  Pallas kernels  54.3 us (36%)
  matrix products  33.1 us (22%)
  starting transfers between devices  20.2 us (13%)
  between operations  14.2 us (9%)
  waiting for transfers between devices  14 us (9%)
  local copies, waits for them, and re-layouts  13 us (9%)
    pallas_call x2, Pallas kernels, gather_small(): pl.pallas_call(functools.partial(gather_kernel, count), out_shape=jax.Sha...  25.9 us
    pallas_call x4, Pallas kernels, call(): pl.pallas_call(kernel, out_shape=outs, in_specs=specs, out_specs=[whole]...  20.2 us
    dot_general x1, matrix products, on_device(): jnp.dot(gated, out_weight, preferred_element_type=F32).astype(BF16)  16.6 us
    dot_general x1, matrix products, on_device(): lax.dot_general(gathered, out_weight, (((1,), (1,)), ((), ())), preferred...  16.4 us
    pallas_call x1, Pallas kernels, weight_grad(): pl.pallas_call(functools.partial(weight_kernel, count), grid=(features //...  8.28 us
    ppermute x7, waiting for transfers between devices, swap(): return lax.ppermute(value, 'ctx', [(i, i ^ k) for i in range(count)])  7.89 us
    ppermute x7, starting transfers between devices, on_device(): lax.ppermute(sums, 'ctx', [(i, i ^ k) for i in range(count)])  7.79 us
    ppermute x7, waiting for transfers between devices, on_device(): lax.ppermute(sums, 'ctx', [(i, i ^ k) for i in range(count)])  5.39 us
  transfers between devices with their start and end apart: 19, of which 5 were waited for; matrix products, arithmetic and copies ran while one was open for 30% of the time, Pallas kernels for 36%

profile of v3, /device:TPU:0, one launch (start us, length us, event | category | flops | bytes accessed | tf_op | source)
XLA Modules:
  0.0 149.5 jit_solution(18340157041020549779)
XLA Ops:
  8.0 1.0 fusion
  8.9 2.4 %collective-permute-start = (bf16[2,3,2048]{2,0,1:T(2,128)(2,1)S(1)}, bf16[2,3,2048]{2,0,1:T(2,128)(2,1)S(1)}, u32[]{:S(2)}, u32[]{:S(2)}) collective-permute-start(bf16[2,3,2048]{2,0,1:T(2,128)(2,1)S(1)} %get-tuple-element.33), channel_id=1, source_target_pairs={{0,4},{4,8},{8,12},{12,16},{16,20},{20,24},{24,28},{1,5},{5,9},{9,... | collective-permute-start | bytes 73736 | tf_op jit(solution)/shard_map/ppermute | solution.py:21
  11.3 1.3 collective-permute-start.1
  19.0 3.0 %local_state.1 = (f32[3,2176,128]{2,1,0:T(8,128)S(1)}, bf16[16,16,128]{2,1,0:T(8,128)(2,1)S(1)}) custom-call(f32[3,136,2048]{2,1,0:T(8,128)S(1)} %convert_bitcast_fusion.ext_ref, f32[58,16,128]{2,1,0:T(8,128)S(1)} %copy-done.1), custom_call_target="tpu_custom_call" | custom-call | flops 8388608 | bytes 7225344 | tf_op jit(solution)/shard_map/local_state/pallas_call | solution.py:443
  22.0 13.2 %gather_states.1.totals_ref = bf16[8,16,16,128]{3,2,1,0:T(8,128)(2,1)S(1)} custom-call(bf16[16,16,128]{2,1,0:T(8,128)(2,1)S(1)} %get-tuple-element.21.block_ref), custom_call_target="tpu_custom_call" | custom-call | bytes 1048576 | tf_op jit(solution)/shard_map/gather_states/pallas_call | solution.py:361
  35.2 5.1 %forward_scan.1 = (bf16[128,2048]{1,0:T(8,128)(2,1)}, f32[2080,128]{1,0:T(8,128)S(1)}) custom-call(s32[1]{0:T(128)} %bitcast.pos_ref, f32[3,2176,128]{2,1,0:T(8,128)S(1)} %get-tuple-element.20.tiles_ref, f32[58,16,128]{2,1,0:T(8,128)S(1)} %copy-done.1, bf16[8,16,16,128]{3,2,1,0:T(8,128)(2,1)S(1)} %gather_states.1.totals_ref), custom_call_target="tpu_custom_call" | custom-call | flops 16777216 | bytes 5931012 | tf_op jit(solution)/shard_map/forward_scan/pallas_call | solution.py:443
  41.3 1.4 collective-permute-start.4
  43.3 1.5 %collective-permute-start.2 = (bf16[128,2048]{1,0:T(8,128)(2,1)}, bf16[128,2048]{1,0:T(8,128)(2,1)}, u32[]{:S(2)}, u32[]{:S(2)}) collective-permute-start(bf16[128,2048]{1,0:T(8,128)(2,1)} %get-tuple-element.22.refs_0_), channel_id=1, source_target_pairs={{0,8},{4,12},{8,0},{12,4},{16,24},{20,28},{24,16},{28,20},{1,9},{5... | collective-permute-start | bytes 1572872 | tf_op jit(solution)/shard_map/ppermute | solution.py:381
  44.8 16.6 %convolution_convert_fusion = bf16[128,8192]{1,0:T(8,128)(2,1)} fusion(bf16[128,2048]{1,0:T(8,128)(2,1)} %get-tuple-element.22.refs_0_, bf16[2048,8192]{1,0:T(8,128)(2,1)} %param.14), kind=kOutput, calls=%fused_computation | convolution fusion | flops 4296015872 | bytes 36175872 | tf_op jit(solution)/shard_map/dot_general | solution.py:498
  61.5 7.1 %collective-permute-done.3.refs_4_ = bf16[128,2048]{1,0:T(8,128)(2,1)} collective-permute-done((bf16[128,2048]{1,0:T(8,128)(2,1)}, bf16[128,2048]{1,0:T(8,128)(2,1)}, u32[]{:S(2)}, u32[]{:S(2)}) %collective-permute-start.3) | collective-permute-done | bytes 524320 | tf_op jit(solution)/shard_map/ppermute | solution.py:381
  68.6 3.1 %copy.25 = bf16[16,8,8,1024]{3,2,0,1:T(8,128)(2,1)} copy(bf16[16,8,8,1024]{3,2,1,0:T(8,128)(2,1)} %bitcast.31) | data formatting | bytes 4194304 | tf_op jit(solution)/shard_map/all_to_all | solution.py:505
  71.8 4.5 %all-to-all-start = ((bf16[128,8,1024]{2,0,1:T(8,128)(2,1)}), bf16[128,8,1024]{2,0,1:T(8,128)(2,1)}, u32[]{:S(2)}, u32[]{:S(2)}) async-start(bf16[128,8,1024]{2,0,1:T(8,128)(2,1)} %bitcast.32), calls=%async_computation.1 | async-start | bytes 4194304 | tf_op jit(solution)/shard_map/all_to_all | solution.py:505
  76.3 16.4 %fusion.2.grad_ref = f32[128,2048]{1,0:T(8,128)S(1)} fusion(bf16[128,8192]{1,0:T(8,128)(2,1)} %all-gather.2.cloned.1.call-done, bf16[2048,8192]{1,0:T(8,128)(2,1)} %param.14), kind=kOutput, calls=%fused_computation.15 | convolution fusion | flops 4294967296 | bytes 36700160 | tf_op jit(solution)/shard_map/dot_general | solution.py:502
  92.8 2.1 %local_adjoint.1 = (f32[2048,128]{1,0:T(8,128)S(1)}, bf16[18,16,128]{2,1,0:T(8,128)(2,1)S(1)}) custom-call(f32[128,2048]{1,0:T(8,128)S(1)} %fusion.2.grad_ref, f32[3,2176,128]{2,1,0:T(8,128)S(1)} %get-tuple-element.20.tiles_ref, f32[58,16,128]{2,1,0:T(8,128)S(1)} %copy-done.2), custom_call_target="tpu_custom_call" | custom-call | flops 8388608 | bytes 5988352 | tf_op jit(solution)/shard_map/local_adjoint/pallas_call | solution.py:443
  94.9 12.7 %gather_adjoints.1.firsts_ref = bf16[8,18,16,128]{3,2,1,0:T(8,128)(2,1)S(1)} custom-call(bf16[18,16,128]{2,1,0:T(8,128)(2,1)S(1)} %get-tuple-element.26.block_ref), custom_call_target="tpu_custom_call" | custom-call | bytes 1179648 | tf_op jit(solution)/shard_map/gather_adjoints/pallas_call | solution.py:361
  107.6 9.9 %backward_scan.1 = (bf16[3,128,2048]{2,1,0:T(8,128)(2,1)}, bf16[26,16,128]{2,1,0:T(8,128)(2,1)S(1)}, f32[32,16,128]{2,1,0:T(8,128)S(1)}) custom-call(s32[1]{0:T(128)} %bitcast.pos_ref, f32[3,2176,128]{2,1,0:T(8,128)S(1)} %get-tuple-element.20.tiles_ref, f32[58,16,128]{2,1,0:T(8,128)S(1)} %copy-done.2, f32[2080,128]{1,0:T(8,128)S(1)} %copy-done.4, ...), custom_call_target="tpu_custom_call" | custom-call | flops 33554432 | bytes 8462340 | tf_op jit(solution)/shard_map/backward_scan/pallas_call | solution.py:443
  117.5 1.3 collective-permute-start.15
  118.9 3.0 %collective-permute-start.14 = (bf16[26,16,128]{2,1,0:T(8,128)(2,1)S(1)}, bf16[26,16,128]{2,1,0:T(8,128)(2,1)S(1)}, u32[]{:S(2)}, u32[]{:S(2)}) collective-permute-start(bf16[26,16,128]{2,1,0:T(8,128)(2,1)S(1)} %get-tuple-element.31), channel_id=1, source_target_pairs={{0,24},{4,28},{8,16},{12,20},{16,8},{20,12},{24,0},{28,4},{1,25},{... | collective-permute-start | bytes 319496 | tf_op jit(solution)/shard_map/ppermute | solution.py:533
  122.5 1.4 collective-permute-start.11
  123.9 1.5 collective-permute-start.10
  125.3 1.0 collective-permute-done.14
  126.4 2.3 %collective-permute-done.13 = bf16[26,16,128]{2,1,0:T(8,128)(2,1)S(1)} collective-permute-done((bf16[26,16,128]{2,1,0:T(8,128)(2,1)S(1)}, bf16[26,16,128]{2,1,0:T(8,128)(2,1)S(1)}, u32[]{:S(2)}, u32[]{:S(2)}) %collective-permute-start.13) | collective-permute-done | bytes 106528 | tf_op jit(solution)/shard_map/ppermute | solution.py:533
  128.6 2.1 %collective-permute-done.12 = bf16[26,16,128]{2,1,0:T(8,128)(2,1)S(1)} collective-permute-done((bf16[26,16,128]{2,1,0:T(8,128)(2,1)S(1)}, bf16[26,16,128]{2,1,0:T(8,128)(2,1)S(1)}, u32[]{:S(2)}, u32[]{:S(2)}) %collective-permute-start.12) | collective-permute-done | bytes 106528 | tf_op jit(solution)/shard_map/ppermute | solution.py:533
  134.4 8.3 %weight_grad.1 = bf16[1024,2048]{1,0:T(8,128)(2,1)} custom-call(s32[1]{0:T(128)} %bitcast.pos_ref, bf16[1024,1024]{1,0:T(8,128)(2,1)} %bitcast.5.columns_ref, bf16[128,2048]{1,0:T(8,128)(2,1)} %get-tuple-element.22.refs_0_, bf16[128,2048]{1,0:T(8,128)(2,1)S(1)} %collective-permute-done.5.refs_1_, bf16[128,2048]{1,0:T(8,128)(2,1)} %collective-permute-done.2.refs_2_, ...), custom_call_target="tpu_custom_call" | custom-call | flops 4294967296 | bytes 10485760 | tf_op jit(solution)/shard_map/weight_grad/pallas_call | solution.py:416
  (57 shorter events, 13.0 us)
Async XLA Ops:
  7.2 10.9 %copy-start.5 = (bf16[128,3,2048]{2,0,1:T(8,128)(2,1)S(1)}, bf16[128,3,2048]{2,0,1:T(8,128)(2,1)}, u32[]{:S(2)}) copy-start(bf16[128,3,2048]{2,0,1:T(8,128)(2,1)} %param.8) | copy-start | bytes 4718596
  7.2 61.4 %all-gather.2.cloned.1.call-start = ((), (), s32[]{:S(2)}) async-start(), calls=%async_computation.3 | async-start | bytes 2621440 | tf_op jit(solution)/shard_map/all_gather | solution.py:468
  7.9 134.7 %reduce-scatter.2.cloned.1.call-start = ((), (), s32[]{:S(2)}) async-start(), calls=%async_computation.2 | async-start | bytes 2621440 | tf_op jit(solution)/shard_map/reduce_scatter | solution.py:500
  8.9 9.1 %collective-permute-start = (bf16[2,3,2048]{2,0,1:T(2,128)(2,1)S(1)}, bf16[2,3,2048]{2,0,1:T(2,128)(2,1)S(1)}, u32[]{:S(2)}, u32[]{:S(2)}) collective-permute-start(bf16[2,3,2048]{2,0,1:T(2,128)(2,1)S(1)} %get-tuple-element.33), channel_id=1, source_target_pairs={{0,4},{4,8},{8,12},{12,16},{16,20},{20,24},{24,28},{1,5},{5,9},{9,... | collective-permute-start | bytes 73736 | tf_op jit(solution)/shard_map/ppermute | solution.py:21
  11.3 6.8 %collective-permute-start.1 = (bf16[2,3,2048]{2,0,1:T(2,128)(2,1)S(1)}, bf16[2,3,2048]{2,0,1:T(2,128)(2,1)S(1)}, u32[]{:S(2)}, u32[]{:S(2)}) collective-permute-start(bf16[2,3,2048]{2,0,1:T(2,128)(2,1)S(1)} %get-tuple-element.34), channel_id=1, source_target_pairs={{4,0},{8,4},{12,8},{16,12},{20,16},{24,20},{28,24},{5,1},{9,5},{13... | collective-permute-start | bytes 73736 | tf_op jit(solution)/shard_map/ppermute | solution.py:21
  18.0 1.1 copy-start.1
  40.4 1.0 copy-start.3
  41.3 20.1 %collective-permute-start.4 = (bf16[128,2048]{1,0:T(8,128)(2,1)}, bf16[128,2048]{1,0:T(8,128)(2,1)}, u32[]{:S(2)}, u32[]{:S(2)}) collective-permute-start(bf16[128,2048]{1,0:T(8,128)(2,1)} %get-tuple-element.22.refs_0_), channel_id=1, source_target_pairs={{0,24},{4,28},{8,16},{12,20},{16,8},{20,12},{24,0},{28,4},{1,25},{... | collective-permute-start | bytes 1572872 | tf_op jit(solution)/shard_map/ppermute | solution.py:381
  42.7 25.8 %collective-permute-start.3 = (bf16[128,2048]{1,0:T(8,128)(2,1)}, bf16[128,2048]{1,0:T(8,128)(2,1)}, u32[]{:S(2)}, u32[]{:S(2)}) collective-permute-start(bf16[128,2048]{1,0:T(8,128)(2,1)} %get-tuple-element.22.refs_0_), channel_id=1, source_target_pairs={{0,16},{4,20},{8,24},{12,28},{16,0},{20,4},{24,8},{28,12},{1,17},{... | collective-permute-start | bytes 1572872 | tf_op jit(solution)/shard_map/ppermute | solution.py:381
  43.3 25.3 %collective-permute-start.2 = (bf16[128,2048]{1,0:T(8,128)(2,1)}, bf16[128,2048]{1,0:T(8,128)(2,1)}, u32[]{:S(2)}, u32[]{:S(2)}) collective-permute-start(bf16[128,2048]{1,0:T(8,128)(2,1)} %get-tuple-element.22.refs_0_), channel_id=1, source_target_pairs={{0,8},{4,12},{8,0},{12,4},{16,24},{20,28},{24,16},{28,20},{1,9},{5... | collective-permute-start | bytes 1572872 | tf_op jit(solution)/shard_map/ppermute | solution.py:381
  71.8 62.6 %all-to-all-start = ((bf16[128,8,1024]{2,0,1:T(8,128)(2,1)}), bf16[128,8,1024]{2,0,1:T(8,128)(2,1)}, u32[]{:S(2)}, u32[]{:S(2)}) async-start(bf16[128,8,1024]{2,0,1:T(8,128)(2,1)} %bitcast.32), calls=%async_computation.1 | async-start | bytes 4194304 | tf_op jit(solution)/shard_map/all_to_all | solution.py:505
  76.3 16.4 %copy-start.2 = (f32[58,16,128]{2,1,0:T(8,128)S(1)}, f32[58,16,128]{2,1,0:T(8,128)}, u32[]{:S(2)}) copy-start(f32[58,16,128]{2,1,0:T(8,128)} %copy-done) | copy-start | bytes 1425412
  92.8 14.9 %copy-start.4 = (f32[2080,128]{1,0:T(8,128)S(1)}, f32[2080,128]{1,0:T(8,128)}, u32[]{:S(2)}) copy-start(f32[2080,128]{1,0:T(8,128)} %copy-done.3) | copy-start | bytes 3194884
  117.5 6.3 %collective-permute-start.15 = (bf16[26,16,128]{2,1,0:T(8,128)(2,1)S(1)}, bf16[26,16,128]{2,1,0:T(8,128)(2,1)S(1)}, u32[]{:S(2)}, u32[]{:S(2)}) collective-permute-start(bf16[26,16,128]{2,1,0:T(8,128)(2,1)S(1)} %get-tuple-element.31), channel_id=1, source_target_pairs={{0,28},{4,24},{8,20},{12,16},{16,12},{20,8},{24,4},{28,0},{1,29},{... | collective-permute-start | bytes 319496 | tf_op jit(solution)/shard_map/ppermute | solution.py:533
  118.9 7.5 %collective-permute-start.14 = (bf16[26,16,128]{2,1,0:T(8,128)(2,1)S(1)}, bf16[26,16,128]{2,1,0:T(8,128)(2,1)S(1)}, u32[]{:S(2)}, u32[]{:S(2)}) collective-permute-start(bf16[26,16,128]{2,1,0:T(8,128)(2,1)S(1)} %get-tuple-element.31), channel_id=1, source_target_pairs={{0,24},{4,28},{8,16},{12,20},{16,8},{20,12},{24,0},{28,4},{1,25},{... | collective-permute-start | bytes 319496 | tf_op jit(solution)/shard_map/ppermute | solution.py:533
  121.8 6.8 %collective-permute-start.13 = (bf16[26,16,128]{2,1,0:T(8,128)(2,1)S(1)}, bf16[26,16,128]{2,1,0:T(8,128)(2,1)S(1)}, u32[]{:S(2)}, u32[]{:S(2)}) collective-permute-start(bf16[26,16,128]{2,1,0:T(8,128)(2,1)S(1)} %get-tuple-element.31), channel_id=1, source_target_pairs={{0,20},{4,16},{8,28},{12,24},{16,4},{20,0},{24,12},{28,8},{1,21},{... | collective-permute-start | bytes 319496 | tf_op jit(solution)/shard_map/ppermute | solution.py:533
  121.8 8.9 %collective-permute-start.12 = (bf16[26,16,128]{2,1,0:T(8,128)(2,1)S(1)}, bf16[26,16,128]{2,1,0:T(8,128)(2,1)S(1)}, u32[]{:S(2)}, u32[]{:S(2)}) collective-permute-start(bf16[26,16,128]{2,1,0:T(8,128)(2,1)S(1)} %get-tuple-element.31), channel_id=1, source_target_pairs={{0,16},{4,20},{8,24},{12,28},{16,0},{20,4},{24,8},{28,12},{1,17},{... | collective-permute-start | bytes 319496 | tf_op jit(solution)/shard_map/ppermute | solution.py:533
  122.5 8.4 %collective-permute-start.11 = (bf16[26,16,128]{2,1,0:T(8,128)(2,1)S(1)}, bf16[26,16,128]{2,1,0:T(8,128)(2,1)S(1)}, u32[]{:S(2)}, u32[]{:S(2)}) collective-permute-start(bf16[26,16,128]{2,1,0:T(8,128)(2,1)S(1)} %get-tuple-element.31), channel_id=1, source_target_pairs={{0,12},{4,8},{8,4},{12,0},{16,28},{20,24},{24,20},{28,16},{1,13},{... | collective-permute-start | bytes 319496 | tf_op jit(solution)/shard_map/ppermute | solution.py:533
  123.9 7.4 %collective-permute-start.10 = (bf16[26,16,128]{2,1,0:T(8,128)(2,1)S(1)}, bf16[26,16,128]{2,1,0:T(8,128)(2,1)S(1)}, u32[]{:S(2)}, u32[]{:S(2)}) collective-permute-start(bf16[26,16,128]{2,1,0:T(8,128)(2,1)S(1)} %get-tuple-element.31), channel_id=1, source_target_pairs={{0,8},{4,12},{8,0},{12,4},{16,24},{20,28},{24,16},{28,20},{1,9},{5... | collective-permute-start | bytes 319496 | tf_op jit(solution)/shard_map/ppermute | solution.py:533
  126.3 5.0 %collective-permute-start.9 = (bf16[26,16,128]{2,1,0:T(8,128)(2,1)S(1)}, bf16[26,16,128]{2,1,0:T(8,128)(2,1)S(1)}, u32[]{:S(2)}, u32[]{:S(2)}) collective-permute-start(bf16[26,16,128]{2,1,0:T(8,128)(2,1)S(1)} %get-tuple-element.31), channel_id=1, source_target_pairs={{0,4},{4,0},{8,12},{12,8},{16,20},{20,16},{24,28},{28,24},{1,5},{5... | collective-permute-start | bytes 319496 | tf_op jit(solution)/shard_map/ppermute | solution.py:533
  128.6 5.0 %collective-permute-start.5 = (bf16[128,2048]{1,0:T(8,128)(2,1)}, bf16[128,2048]{1,0:T(8,128)(2,1)S(1)}, u32[]{:S(2)}, u32[]{:S(2)}) collective-permute-start(bf16[128,2048]{1,0:T(8,128)(2,1)} %get-tuple-element.22.refs_0_), channel_id=1, source_target_pairs={{0,4},{4,0},{8,12},{12,8},{16,20},{20,16},{24,28},{28,24},{1,5},{5... | collective-permute-start | bytes 1572872 | tf_op jit(solution)/shard_map/ppermute | solution.py:381
  130.7 2.9 %collective-permute-start.6 = (bf16[128,2048]{1,0:T(8,128)(2,1)}, bf16[128,2048]{1,0:T(8,128)(2,1)S(1)}, u32[]{:S(2)}, u32[]{:S(2)}) collective-permute-start(bf16[128,2048]{1,0:T(8,128)(2,1)} %collective-permute-done.2.refs_2_), channel_id=1, source_target_pairs={{0,4},{4,0},{8,12},{12,8},{16,20},{20,16},{24,28},{28,24},{1,5},{5... | collective-permute-start | bytes 1572872 | tf_op jit(solution)/shard_map/ppermute | solution.py:381
  130.8 2.8 %collective-permute-start.7 = (bf16[128,2048]{1,0:T(8,128)(2,1)}, bf16[128,2048]{1,0:T(8,128)(2,1)S(1)}, u32[]{:S(2)}, u32[]{:S(2)}) collective-permute-start(bf16[128,2048]{1,0:T(8,128)(2,1)} %collective-permute-done.3.refs_4_), channel_id=1, source_target_pairs={{0,4},{4,0},{8,12},{12,8},{16,20},{20,16},{24,28},{28,24},{1,5},{5... | collective-permute-start | bytes 1572872 | tf_op jit(solution)/shard_map/ppermute | solution.py:381
  131.2 3.1 %collective-permute-start.8 = (bf16[128,2048]{1,0:T(8,128)(2,1)}, bf16[128,2048]{1,0:T(8,128)(2,1)S(1)}, u32[]{:S(2)}, u32[]{:S(2)}) collective-permute-start(bf16[128,2048]{1,0:T(8,128)(2,1)} %collective-permute-done.4.refs_6_), channel_id=1, source_target_pairs={{0,4},{4,0},{8,12},{12,8},{16,20},{20,16},{24,28},{28,24},{1,5},{5... | collective-permute-start | bytes 1572872 | tf_op jit(solution)/shard_map/ppermute | solution.py:381
  (1 other events, 0.8 us)
Sparse Core Ops, SparseCore 0:
  9.6 48.6 all-gather.1
  68.7 44.0 reduce-scatter.1
